TPU v7x, 128 devices: a whole 4x4x4 slice. The times are simulated.
128 devices in a mesh: req: 8 (over z, x_hi), head: 16 (over x_lo, y, core).
Axes of the slice: x: 4 (x_hi: 2, x_lo: 2; x = x_hi * 2 + x_lo), y: 4, z: 4, core: 2. Of those that a mesh axis runs over, the one named last changes fastest.
Arguments:
- tokens: bfloat16 [8192, 2048], P(('req', 'head')), may hold values from -6 to 6
- in_gain: float32 [2, 2048], replicated, may hold values from 0.25 to 1.75
- w_query: bfloat16 [2, 2048, 2048], P(None, None, 'head'), may hold values from -0.125 to 0.125
- w_key: bfloat16 [2, 2048, 2048], P(None, None, 'head'), may hold values from -0.125 to 0.125
- w_value: bfloat16 [2, 2048, 4096], P(None, None, 'head'), may hold values from -0.125 to 0.125
- w_gate_z: bfloat16 [2, 2048, 4096], P(None, None, 'head'), may hold values from -0.125 to 0.125
- w_beta: bfloat16 [2, 2048, 32], P(None, None, 'head'), may hold values from -0.125 to 0.125
- w_decay: bfloat16 [2, 2048, 32], P(None, None, 'head'), may hold values from -0.125 to 0.125
- conv_query: float32 [2, 4, 2048], P(None, None, 'head'), may hold values from -3 to 3
- conv_key: float32 [2, 4, 2048], P(None, None, 'head'), may hold values from -3 to 3
- conv_value: float32 [2, 4, 4096], P(None, None, 'head'), may hold values from -3 to 3
- a_log: float32 [2, 32], P(None, 'head'), may hold values from -4 to 0.5
- dt_bias: float32 [2, 32], P(None, 'head'), may hold values from -4 to 0
- out_gain: float32 [2, 128], replicated, may hold values from 0.25 to 1.75
- w_out: bfloat16 [2, 4096, 2048], P(None, 'head'), may hold values from -0.09375 to 0.09375
- state_pool: float32 [32, 32, 128, 128], P('req', 'head'), may hold values from -6 to 6
- hit_owner: int32 [16, 2], P('req'), may hold values from 0 to 7, as said below
- hit_slot: int32 [16, 2], P('req'), may hold values from 0 to 3
- lengths: int32 [16], P('req'), may hold values from 1 to 512, as said below
Outputs:
- out_rows: bfloat16 [8192, 2048], P(('req', 'head'))
- final_states: float32 [16, 2, 32, 128, 128], P('req', None, 'head')
Inputs may be any that keep to these rules, and one draw needn't show every extreme that they name: Request r's layer-l state is pool row hit_owner * 4 + hit_slot; every pool row is named by exactly one (request, layer); among the entries of the requests of one index of req at most 2 share an owner, and 2 do in every draw. `lengths`: some request has exactly 512 valid tokens.
All inputs are finite; a program needn't handle non-finite values.
Results may differ from a plain program's by a relative error of at most 0.025.
Values may be sent and summed in bfloat16 or wider, within the bound.
A program may use at most 128 MiB of HBM per device.

v0:
```python
import jax
import jax.numpy as jnp
from jax import lax
from jax.sharding import PartitionSpec as P

DK = 128
DV = 128
L = 2
BLOCK = 64
SLOTS = 4


EPS = 1e-06
PRECISE = lax.Precision.HIGHEST


def normalize(token_rows, gain):
    floats = token_rows.astype(jnp.float32)
    return floats * lax.rsqrt(jnp.mean(floats * floats, -1, keepdims=True) + EPS) * gain


def project(normed, weights):
    return jnp.concatenate(
        [jnp.dot(normed, weight, preferred_element_type=jnp.float32) for weight in weights], 1
    )


def causal_conv(signal, kernel):
    kernel_taps = kernel.shape[0]
    length = signal.shape[1]
    padded = jnp.pad(signal, ((0, 0), (kernel_taps - 1, 0), (0, 0)))
    summed = padded[:, 0:length, :] * kernel[0]
    for offset in range(1, kernel_taps):
        summed = summed + padded[:, offset : offset + length, :] * kernel[offset]
    return summed


def unit_rows(vectors):
    return vectors * lax.rsqrt(jnp.sum(vectors * vectors, -1, keepdims=True) + EPS)


def unit_lower_inverse(strict_part):
    negated = -strict_part
    identity = jnp.eye(strict_part.shape[-1], dtype=jnp.float32)
    inverse = identity + negated
    power = negated
    for level in range(strict_part.shape[-1].bit_length() - 2):
        power = jnp.einsum("bnij,bnjk->bnik", power, power, precision=PRECISE)
        inverse = inverse + jnp.einsum("bnij,bnjk->bnik", inverse, power, precision=PRECISE)
    return inverse


def delta_blocks(queries, key_vecs, values, beta_gate, log_decay, state_init):
    batch, length, kdim = key_vecs.shape
    vdim = values.shape[2]
    blocks = length // BLOCK
    query_b = queries.reshape(batch, blocks, BLOCK, kdim)
    key_b = key_vecs.reshape(batch, blocks, BLOCK, kdim)
    value_b = values.reshape(batch, blocks, BLOCK, vdim)
    beta_b = beta_gate.reshape(batch, blocks, BLOCK)
    cumul = jnp.cumsum(log_decay.reshape(batch, blocks, BLOCK), -1)
    ranks = jnp.arange(BLOCK, dtype=jnp.int32)
    lower = ranks[:, None] >= ranks[None, :]
    strict = ranks[:, None] > ranks[None, :]
    spread = cumul[..., :, None] - cumul[..., None, :]
    decays = jnp.where(lower, jnp.exp(jnp.where(lower, spread, 0.0)), 0.0)
    key_dots = jnp.einsum("bnik,bnjk->bnij", key_b, key_b, precision=PRECISE)
    strict_part = jnp.where(strict, key_dots * decays * beta_b[..., :, None], 0.0)
    inverse = unit_lower_inverse(strict_part)
    right_side = jnp.concatenate(
        [value_b * beta_b[..., None], key_b * (beta_b * jnp.exp(cumul))[..., None]], -1
    )
    solved = jnp.einsum("bnij,bnjc->bnic", inverse, right_side, precision=PRECISE)
    plain_part = solved[..., :vdim]
    state_part = solved[..., vdim:]
    mixing = jnp.einsum("bnik,bnjk->bnij", query_b, key_b, precision=PRECISE) * decays
    query_decay = query_b * jnp.exp(cumul)[..., None]
    key_tail = key_b * jnp.exp(cumul[..., -1:] - cumul)[..., None]
    tail_decay = jnp.exp(cumul[..., -1])

    def advance(state, pieces):
        plain_now, state_now, mixing_now, query_now, tail_keys, tail_now = pieces
        update = plain_now - jnp.einsum("bik,bkv->biv", state_now, state, precision=PRECISE)
        output = jnp.einsum("bik,bkv->biv", query_now, state, precision=PRECISE)
        output = output + jnp.einsum("bij,bjv->biv", mixing_now, update, precision=PRECISE)
        state = tail_now[:, None, None] * state + jnp.einsum(
            "bik,biv->bkv", tail_keys, update, precision=PRECISE
        )
        return (state, output)

    moved = tuple(
        (
            jnp.moveaxis(array, 1, 0)
            for array in (plain_part, state_part, mixing, query_decay, key_tail, tail_decay)
        )
    )
    final, outputs = lax.scan(advance, state_init, moved)
    outputs = jnp.moveaxis(outputs, 0, 1).reshape(batch, length, vdim)
    return (outputs, final)


def mixer(projected, kernels, rates, head_gain, state_init, lengths, key_width, value_width):
    requests = lengths.shape[0]
    length = projected.shape[0] // requests
    key_heads = key_width // DK
    value_heads = value_width // DV
    cuts = [
        0,
        key_width,
        2 * key_width,
        2 * key_width + value_width,
        2 * key_width + 2 * value_width,
        2 * key_width + 2 * value_width + value_heads,
        2 * key_width + 2 * value_width + 2 * value_heads,
    ]
    pieces = [
        projected[:, cuts[part] : cuts[part + 1]].reshape(
            requests, length, cuts[part + 1] - cuts[part]
        )
        for part in range(6)
    ]
    queries = jax.nn.silu(causal_conv(pieces[0], kernels[0])).reshape(
        requests, length, key_heads, DK
    )
    queries = unit_rows(queries) * DK ** (-0.5)
    key_vecs = unit_rows(
        jax.nn.silu(causal_conv(pieces[1], kernels[1])).reshape(requests, length, key_heads, DK)
    )
    values = jax.nn.silu(causal_conv(pieces[2], kernels[2])).reshape(
        requests, length, value_heads, DV
    )
    gate_z = pieces[3].reshape(requests, length, value_heads, DV)
    positions = jnp.arange(length, dtype=jnp.int32)
    valid = positions[None, :] < lengths[:, None]
    beta_gate = jnp.where(valid[..., None], jax.nn.sigmoid(pieces[4]), 0.0)
    log_decay = jnp.where(
        valid[..., None], -jnp.exp(rates[0]) * jax.nn.softplus(pieces[5] + rates[1]), 0.0
    )
    queries = jnp.repeat(queries, value_heads // key_heads, axis=2)
    key_vecs = jnp.repeat(key_vecs, value_heads // key_heads, axis=2)

    def flatten(array):
        return jnp.moveaxis(array, 2, 1).reshape(requests * value_heads, length, array.shape[3])

    def flatten_gate(array):
        return jnp.moveaxis(array, 2, 1).reshape(requests * value_heads, length)

    outputs, final = delta_blocks(
        flatten(queries),
        flatten(key_vecs),
        flatten(values),
        flatten_gate(beta_gate),
        flatten_gate(log_decay),
        state_init.reshape(requests * value_heads, DK, DV),
    )
    outputs = jnp.moveaxis(outputs.reshape(requests, value_heads, length, DV), 1, 2)
    scaled = outputs * lax.rsqrt(jnp.mean(outputs * outputs, -1, keepdims=True) + EPS) * head_gain
    scaled = scaled * jax.nn.silu(gate_z) * valid[..., None, None].astype(jnp.float32)
    return (
        scaled.reshape(requests * length, value_heads * DV).astype(jnp.bfloat16),
        final.reshape(requests, value_heads, DK, DV),
    )


def on_device(
    tokens,
    in_gain,
    w_query,
    w_key,
    w_value,
    w_gate_z,
    w_beta,
    w_decay,
    conv_query,
    conv_key,
    conv_value,
    a_log,
    dt_bias,
    out_gain,
    w_out,
    state_pool,
    hit_owner,
    hit_slot,
    lengths,
):
    key_width = w_query.shape[2]
    value_width = w_value.shape[2]
    requests = lengths.shape[0]
    head_count = state_pool.shape[1]
    wanted = (hit_owner * SLOTS + hit_slot).reshape(-1)
    empty = jnp.zeros((wanted.shape[0], head_count * DK * DV), jnp.float32)
    piece = lax.all_gather(state_pool.astype(jnp.bfloat16), "req", axis=0, tiled=True).astype(
        jnp.float32
    )
    count = piece.shape[0]
    chosen = (wanted[:, None] == jnp.arange(count, dtype=jnp.int32)[None, :]).astype(jnp.float32)
    picked = empty + jnp.dot(chosen, piece.reshape(count, -1), precision=PRECISE)
    starts = picked.reshape(requests, L, head_count, DK, DV)

    def layer_weights(level):
        return (
            w_query[level],
            w_key[level],
            w_value[level],
            w_gate_z[level],
            w_beta[level],
            w_decay[level],
        )

    def run_mixer(projected, level):
        return mixer(
            projected,
            (conv_query[level], conv_key[level], conv_value[level]),
            (a_log[level], dt_bias[level]),
            out_gain[level],
            starts[:, level],
            lengths,
            key_width,
            value_width,
        )

    def gather_projected(rows_in, level):
        normed = normalize(rows_in, in_gain[level]).astype(jnp.bfloat16)
        return project(lax.all_gather(normed, "head", axis=0, tiled=True), layer_weights(level))

    def reduce_branch(mixed, level):
        return lax.psum_scatter(
            jnp.dot(mixed, w_out[level], preferred_element_type=jnp.float32).astype(jnp.bfloat16),
            "head",
            scatter_dimension=0,
            tiled=True,
        ).astype(jnp.float32)

    mixed, first_end = run_mixer(gather_projected(tokens, 0), 0)
    current = (tokens.astype(jnp.float32) + reduce_branch(mixed, 0)).astype(jnp.bfloat16)
    projected = gather_projected(current, 1)
    mixed, second_end = run_mixer(projected, 1)
    result = (current.astype(jnp.float32) + reduce_branch(mixed, 1)).astype(jnp.bfloat16)
    return (result, jnp.stack([first_end, second_end], 1))


def solution(mesh):
    in_specs = (
        P(("req", "head"), None),
        P(),
        P(None, None, "head"),
        P(None, None, "head"),
        P(None, None, "head"),
        P(None, None, "head"),
        P(None, None, "head"),
        P(None, None, "head"),
        P(None, None, "head"),
        P(None, None, "head"),
        P(None, None, "head"),
        P(None, "head"),
        P(None, "head"),
        P(),
        P(None, "head", None),
        P("req", "head", None, None),
        P("req", None),
        P("req", None),
        P("req"),
    )
    out_specs = (P(("req", "head"), None), P("req", None, "head", None, None))
    return jax.shard_map(
        on_device, mesh=mesh, in_specs=in_specs, out_specs=out_specs, check_vma=False
    )
```

profile of v0, /device:TPU:2, one launch (start us, length us, event | category | flops | bytes accessed | tf_op | source)
XLA Modules:
  0.0 462.3 jit_solution(3732658367289413070)
XLA Ops:
  7.3 1.8 convert_element_type.77
  11.1 1.8 fusion.79
  13.0 2.7 slice_bitcast_fusion.4
  15.6 1.5 copy.71
  17.4 49.3 %all-gather.4.cloned.1.call-done = bf16[32,2,128,128]{3,2,1,0:T(8,128)(2,1)} async-done(((bf16[4,2,128,128]{3,2,1,0:T(8,128)(2,1)}), bf16[32,2,128,128]{3,2,1,0:T(8,128)(2,1)}) %all-gather.4.cloned.1.call-update) | async-done | bytes 2097168 | tf_op jit(solution)/shard_map/all_gather | solution.py:192
  66.7 2.9 copy.113
  71.8 32.9 %all-gather.6.cloned.1.call-done = bf16[1024,2048]{1,0:T(8,128)(2,1)} async-done(((bf16[64,2048]{1,0:T(8,128)(2,1)}), bf16[1024,2048]{1,0:T(8,128)(2,1)}) %all-gather.6.cloned.1.call-update) | async-done | bytes 4194320 | tf_op jit(solution)/shard_map/all_gather | solution.py:224
  104.7 3.6 fusion.95
  110.1 3.4 fusion.61
  115.2 1.9 fusion.48
  126.9 2.7 convolution_add_fusion.10
  130.9 1.6 divide_multiply_fusion.1
  132.5 2.8 reshape.324
  135.3 1.4 copy.63
  138.2 1.6 broadcast_multiply_fusion.2
  139.8 1.9 fusion.32
  141.8 1.7 slice_bitcast_fusion.2
  145.4 1.8 fusion.45
  147.2 1.3 multiply_bitcast_fusion.2
  148.8 36.0 %while.24 = (s32[]{:T(128)}, f32[4,128,128]{2,1,0:T(8,128)S(1)}, f32[8,4,64,128]{3,2,1,0:T(8,128)S(1)}, f32[8,4]{1,0:T(8,128)S(1)}, f32[8,4,64,128]{3,2,0,1:T(8,...) while((s32[]{:T(128)}, f32[4,128,128]{2,1,0:T(8,128)S(1)}, ...), condition=%wide.region_5.6_spmd, body=%wide.region_4.5_spmd.sunk | while | flops 176357376 | bytes 2493085 | solution.py:97
  148.9 1.3 convolution_subtract_fusion.4
  151.9 1.5 convolution_add_fusion.18
  153.4 1.3 convolution_subtract_fusion.4
  156.3 1.5 convolution_add_fusion.18
  157.9 1.3 convolution_subtract_fusion.4
  160.8 1.5 convolution_add_fusion.18
  162.4 1.3 convolution_subtract_fusion.4
  165.3 1.5 convolution_add_fusion.18
  166.8 1.3 convolution_subtract_fusion.4
  169.8 1.5 convolution_add_fusion.18
  171.3 1.3 convolution_subtract_fusion.4
  174.2 1.5 convolution_add_fusion.18
  175.8 1.3 convolution_subtract_fusion.4
  178.7 1.5 convolution_add_fusion.18
  180.3 1.3 convolution_subtract_fusion.4
  183.2 1.5 convolution_add_fusion.18
  185.2 4.1 multiply_convert_fusion.1
  189.9 3.2 convolution_convert_fusion.1
  193.2 66.2 %reduce-scatter.3.cloned.1.call-done = bf16[64,2048]{1,0:T(8,128)(2,1)} async-done(((bf16[1024,2048]{1,0:T(8,128)(2,1)}), bf16[64,2048]{1,0:T(8,128)(2,1)}) %reduce-scatter.3.cloned.1.call-update) | async-done | bytes 262160 | tf_op jit(solution)/shard_map/reduce_scatter | solution.py:227
  260.6 1.8 fusion.83
  262.4 1.4 copy.81
  263.9 35.2 %all-gather.8.cloned.1.call-done = bf16[1024,2048]{1,0:T(8,128)(2,1)} async-done(((bf16[64,2048]{1,0:T(8,128)(2,1)}), bf16[1024,2048]{1,0:T(8,128)(2,1)}) %all-gather.8.cloned.1.call-update) | async-done | bytes 4194320 | tf_op jit(solution)/shard_map/all_gather | solution.py:224
  299.0 3.7 fusion.89
  302.8 2.4 fusion.91
  306.4 2.3 fusion.64
  312.1 1.9 fusion.50
  315.1 2.3 convolution_add_fusion.8
  319.5 2.8 fusion.43
  322.3 1.3 multiply_bitcast_fusion
  323.6 1.7 divide_multiply_fusion
  325.3 2.7 reshape.325
  328.0 1.4 copy.73
  330.9 1.6 convolution_add_fusion.7
  339.2 1.9 fusion.36
  341.2 1.7 slice_bitcast_fusion
  343.1 35.9 %while.25 = (s32[]{:T(128)}, f32[4,128,128]{2,1,0:T(8,128)S(1)}, f32[8,4,64,128]{3,2,1,0:T(8,128)S(1)}, f32[8,4]{1,0:T(8,128)S(1)}, f32[8,4,64,128]{3,2,0,1:T(8,...) while((s32[]{:T(128)}, f32[4,128,128]{2,1,0:T(8,128)S(1)}, ...), condition=%wide.region_13.14_spmd, body=%wide.region_12.13_spmd.sunk | while | flops 176357376 | bytes 2493581 | solution.py:97
  343.1 1.3 convolution_subtract_fusion.5
  347.5 1.3 convolution_subtract_fusion.5
  352.0 1.3 convolution_subtract_fusion.5
  356.5 1.3 convolution_subtract_fusion.5
  379.5 4.1 multiply_convert_fusion
  384.2 3.2 convolution_convert_fusion
  388.2 65.6 %reduce-scatter.5.cloned.1.call-done = bf16[64,2048]{1,0:T(8,128)(2,1)} async-done(((bf16[1024,2048]{1,0:T(8,128)(2,1)}), bf16[64,2048]{1,0:T(8,128)(2,1)}) %reduce-scatter.5.cloned.1.call-update) | async-done | bytes 262160 | tf_op jit(solution)/shard_map/reduce_scatter | solution.py:227
  453.8 1.7 fusion.84
  (207 shorter events, 85.1 us)
Async XLA Ops:
  7.2 10.0 %copy-start.19 = (f32[2,128]{1,0:T(2,128)S(1)}, f32[2,128]{1,0:T(2,128)}, u32[]{:S(2)}) copy-start(f32[2,128]{1,0:T(2,128)} %param.36) | copy-start | bytes 3076
  7.2 10.0 %copy-start.18 = (s32[2,2]{1,0:T(2,128)S(1)}, s32[2,2]{1,0:T(2,128)}, u32[]{:S(2)}) copy-start(s32[2,2]{1,0:T(2,128)} %param.39) | copy-start | bytes 52
  7.2 10.0 %copy-start.17 = (s32[2,2]{1,0:T(2,128)S(1)}, s32[2,2]{1,0:T(2,128)}, u32[]{:S(2)}) copy-start(s32[2,2]{1,0:T(2,128)} %param.40) | copy-start | bytes 52
  7.2 10.0 %copy-start.21 = (f32[2,2]{1,0:T(2,128)S(1)}, f32[2,2]{1,0:T(2,128)}, u32[]{:S(2)}) copy-start(f32[2,2]{1,0:T(2,128)} %param.34) | copy-start | bytes 52
  7.2 10.0 %copy-start.20 = (f32[2,2]{1,0:T(2,128)S(1)}, f32[2,2]{1,0:T(2,128)}, u32[]{:S(2)}) copy-start(f32[2,2]{1,0:T(2,128)} %param.35) | copy-start | bytes 52
  7.2 10.0 %copy-start.15 = (f32[2,4,128]{2,1,0:T(4,128)S(1)}, f32[2,4,128]{2,1,0:T(4,128)}, u32[]{:S(2)}) copy-start(f32[2,4,128]{2,1,0:T(4,128)} %param.32) | copy-start | bytes 12292
  7.2 10.0 %copy-start.16 = (f32[2,4,128]{2,1,0:T(4,128)S(1)}, f32[2,4,128]{2,1,0:T(4,128)}, u32[]{:S(2)}) copy-start(f32[2,4,128]{2,1,0:T(4,128)} %param.31) | copy-start | bytes 12292
  7.2 10.0 %copy-start.22 = (s32[2]{0:T(128)S(1)}, s32[2]{0:T(128)}, u32[]{:S(2)}) copy-start(s32[2]{0:T(128)} %param.41) | copy-start | bytes 28
  7.2 10.1 %copy-start.14 = (f32[2,4,256]{2,1,0:T(4,128)S(1)}, f32[2,4,256]{2,1,0:T(4,128)}, u32[]{:S(2)}) copy-start(f32[2,4,256]{2,1,0:T(4,128)} %param.33) | copy-start | bytes 24580
  7.3 59.4 %all-gather.4.cloned.1.call-start = ((), (), s32[]{:S(2)}) async-start(), calls=%async_computation.2 | async-start | bytes 2359296 | tf_op jit(solution)/shard_map/all_gather | solution.py:192
  9.1 95.6 %all-gather.6.cloned.1.call-start = ((), (), s32[]{:S(2)}) async-start(), calls=%async_computation.3 | async-start | bytes 4456448 | tf_op jit(solution)/shard_map/all_gather | solution.py:224
  12.9 246.5 %reduce-scatter.3.cloned.1.call-start = ((), (), s32[]{:S(2)}) async-start(), calls=%async_computation.4 | async-start | bytes 4456448 | tf_op jit(solution)/shard_map/reduce_scatter | solution.py:227
  69.6 35.1 %copy-start.26 = (bf16[2,2048,128]{2,1,0:T(8,128)(2,1)S(1)}, bf16[2,2048,128]{2,1,0:T(8,128)(2,1)}, u32[]{:S(2)}) copy-start(bf16[2,2048,128]{2,1,0:T(8,128)(2,1)} %param.26) | copy-start | bytes 3145732
  71.4 37.3 %copy-start.13 = (bf16[2,2048,2]{1,2,0:T(2,128)(2,1)S(1)}, bf16[2,2048,2]{1,2,0:T(2,128)(2,1)}, u32[]{:S(2)}) copy-start(bf16[2,2048,2]{1,2,0:T(2,128)(2,1)} %param.30) | copy-start | bytes 49156
  104.7 4.1 copy-start
  104.7 5.4 %copy-start.12 = (bf16[2,2048,2]{1,2,0:T(2,128)(2,1)S(1)}, bf16[2,2048,2]{1,2,0:T(2,128)(2,1)}, u32[]{:S(2)}) copy-start(bf16[2,2048,2]{1,2,0:T(2,128)(2,1)} %param.29) | copy-start | bytes 49156
  124.5 5.2 %copy-start.1 = (bf16[1024,2048]{1,0:T(8,128)(2,1)S(1)}, bf16[1024,2048]{1,0:T(8,128)(2,1)}, u32[]{:S(2)}) copy-start(bf16[1024,2048]{1,0:T(8,128)(2,1)} %all-gather.6.cloned.1.call-done) | copy-start | bytes 12582916
  124.5 5.1 %copy-start.23 = (bf16[2,2048,256]{2,1,0:T(8,128)(2,1)S(1)}, bf16[2,2048,256]{2,1,0:T(8,128)(2,1)}, u32[]{:S(2)}) copy-start(bf16[2,2048,256]{2,1,0:T(8,128)(2,1)} %param.27) | copy-start | bytes 6291460
  135.3 1.7 copy-start.6
  139.8 3.6 copy-start.2
  139.8 3.6 copy-start.25
  185.2 4.7 %copy-start.9 = (bf16[2,256,2048]{2,1,0:T(8,128)(2,1)S(1)}, bf16[2,256,2048]{2,1,0:T(8,128)(2,1)}, u32[]{:S(2)}) copy-start(bf16[2,256,2048]{2,1,0:T(8,128)(2,1)} %param.37) | copy-start | bytes 6291460
  189.9 69.5 %copy-start.4 = (bf16[64,2048]{1,0:T(8,128)(2,1)S(1)}, bf16[64,2048]{1,0:T(8,128)(2,1)}, u32[]{:S(2)}) copy-start(bf16[64,2048]{1,0:T(8,128)(2,1)} %param.23) | copy-start | bytes 786436
  193.1 69.3 %copy-start.7 = (bf16[256,2048]{0,1:T(8,128)(2,1)S(1)}, bf16[256,2048]{0,1:T(8,128)(2,1)}, u32[]{:S(2)}) copy-start(bf16[256,2048]{0,1:T(8,128)(2,1)} %get-tuple-element.202) | copy-start | bytes 3145732
  193.2 105.9 %all-gather.8.cloned.1.call-start = ((), (), s32[]{:S(2)}) async-start(), calls=%async_computation.5 | async-start | bytes 4456448 | tf_op jit(solution)/shard_map/all_gather | solution.py:224
  262.4 191.4 %reduce-scatter.5.cloned.1.call-start = ((), (), s32[]{:S(2)}) async-start(), calls=%async_computation.6 | async-start | bytes 4456448 | tf_op jit(solution)/shard_map/reduce_scatter | solution.py:227
  299.0 3.7 copy-start.3
  302.7 3.7 copy-start.24
  319.2 4.4 copy-start.11
  328.0 2.9 copy-start.5
  379.5 4.7 %copy-start.10 = (bf16[2,256,2048]{2,1,0:T(8,128)(2,1)S(1)}, bf16[2,256,2048]{2,1,0:T(8,128)(2,1)}, u32[]{:S(2)}) copy-start(bf16[2,256,2048]{2,1,0:T(8,128)(2,1)} %param.37) | copy-start | bytes 6291460
  387.4 66.4 %copy-start.8 = (bf16[64,2048]{1,0:T(8,128)(2,1)S(1)}, bf16[64,2048]{1,0:T(8,128)(2,1)}, u32[]{:S(2)}) copy-start(bf16[64,2048]{1,0:T(8,128)(2,1)} %reduce-scatter.3.cloned.1.call-done) | copy-start | bytes 786436
Sparse Core Ops, SparseCore 0:
  11.0 55.5 all-gather.3
  68.9 35.7 all-gather.5
  193.3 66.0 reduce-scatter.2
  262.5 36.4 all-gather.7
  387.5 66.2 reduce-scatter.4
where the time goes:
time: 470 us; the launch traced here: 462 us
  waiting for transfers between devices  249 us (53%)
  matrix products  147 us (31%)
  other arithmetic  24.8 us (5%)
  local copies, waits for them, and re-layouts  24.7 us (5%)
  between operations  14.8 us (3%)
    reduce_scatter x2, waiting for transfers between devices, reduce_branch(): lax.psum_scatter(jnp.dot(mixed, w_out[level], preferred_element_type=jnp....  132 us
    all_gather x2, waiting for transfers between devices, gather_projected(): lax.all_gather(normed, 'head', axis=0, tiled=True)  68 us
    all_gather x1, waiting for transfers between devices, on_device(): lax.all_gather(state_pool.astype(jnp.bfloat16), 'req', axis=0, tiled=True)  49.3 us
    dot_general x12, matrix products, project(): jnp.dot(normed, weight, preferred_element_type=jnp.float32)  29.8 us
    dot_general x16, matrix products, advance(): jnp.einsum('bik,bkv->biv', state_now, state, precision=PRECISE)  21.3 us
    dot_general x16, matrix products, advance(): output = jnp.einsum('bik,bkv->biv', query_now, state, precision=PRECISE)  20.3 us
    dot_general x16, matrix products, advance(): jnp.einsum('bik,biv->bkv', tail_keys, update, precision=PRECISE)  17.5 us
    dot_general x10, matrix products, unit_lower_inverse(): jnp.einsum('bnij,bnjk->bnik', inverse, power, precision=PRECISE)  15.2 us
  transfers between devices with their start and end apart: 5, of which 5 were waited for; matrix products, arithmetic and copies ran while one was open for 3% of the time, Pallas kernels for 0%

commit v1 on v0

v1 whole, which is shorter than its diff:
```python
import jax
import jax.numpy as jnp
from jax import lax
from jax.experimental import pallas as pl
from jax.experimental.pallas import tpu as pltpu
from jax.sharding import PartitionSpec as P

DK = 128
DV = 128
L = 2
SLOTS = 4
SUF = 512
CONV = 4
HEADS = 2
CHUNK = 128
BLOCKS = SUF // CHUNK
PAD = 8
EPS = 1e-06
BF = jnp.bfloat16
F32 = jnp.float32
PRECISE = lax.Precision.HIGHEST


def silu(v):
    return v / (1.0 + jnp.exp(-v))


def conv_block(ref, row, width, taps, tap_col):
    window = ref[pl.ds(row, CHUNK + PAD), 0:width]
    total = None
    for tap in range(CONV):
        first = PAD - (CONV - 1) + tap
        term = window[first : first + CHUNK] * taps[tap : tap + 1, tap_col : tap_col + width]
        total = term if total is None else total + term
    return silu(total)


def unit_rows(vectors):
    return vectors * lax.rsqrt(jnp.sum(vectors * vectors, -1, keepdims=True) + EPS)


def mm(a, b):
    return jnp.dot(a.astype(BF), b.astype(BF), preferred_element_type=F32)


def nt(a, b):
    return lax.dot_general(
        a.astype(BF), b.astype(BF), (((1,), (1,)), ((), ())), preferred_element_type=F32
    )


def lower_inverse(strict, rows, cols):
    size = 16
    diag = jnp.where(rows // size == cols // size, -strict, 0.0)
    inverse = jnp.where(rows == cols, 1.0, 0.0) + diag
    power = mm(diag, diag)
    for _ in range(2):
        both = mm(jnp.concatenate([power, inverse], 0), power)
        inverse = inverse + both[CHUNK:]
        power = both[:CHUNK]
    inverse = inverse + mm(inverse, power)
    while size < CHUNK:
        joined = (rows // (2 * size) == cols // (2 * size)) & (rows // size > cols // size)
        corner = jnp.where(joined, strict, 0.0)
        inverse = inverse - mm(inverse, mm(corner, inverse))
        size *= 2
    return inverse


def gate_rows(raw, a_log, dt_bias, length):
    valid = lax.broadcasted_iota(jnp.int32, (1, SUF), 1) < length
    rows = []
    for head in range(HEADS):
        rows.append(jnp.where(valid, 1.0 / (1.0 + jnp.exp(-raw[head : head + 1])), 0.0))
    for head in range(HEADS):
        shifted = raw[HEADS + head : HEADS + head + 1] + dt_bias[head]
        soft = jnp.maximum(shifted, 0.0) + jnp.log1p(jnp.exp(-jnp.abs(shifted)))
        rate = jnp.exp(jnp.full((1, SUF), a_log[head], F32))
        rows.append(jnp.where(valid, -rate * soft, 0.0))
    rows.append(jnp.zeros((8 - 2 * HEADS, SUF), F32))
    return jnp.concatenate(rows, 0)


def block_terms(block, q_ref, k_ref, v_ref, taps, gates, move_ref, add_ref, tail_ref):
    row = block * CHUNK
    rows = lax.broadcasted_iota(jnp.int32, (CHUNK, CHUNK), 0)
    cols = lax.broadcasted_iota(jnp.int32, (CHUNK, CHUNK), 1)
    upper = jnp.where(rows <= cols, 1.0, 0.0)
    sums = jnp.dot(gates, upper, precision=lax.Precision.HIGHEST, preferred_element_type=F32)
    columns = jnp.concatenate([gates, sums], 0).T
    queries = unit_rows(conv_block(q_ref, row, DK, taps, 0)) * DK ** (-0.5)
    keys = unit_rows(conv_block(k_ref, row, DK, taps, DK))
    values = conv_block(v_ref, row, HEADS * DV, taps, 2 * DK)
    dots = nt(jnp.concatenate([keys, queries], 0), keys)
    for head in range(HEADS):
        beta = columns[:, head : head + 1]
        cumul = columns[:, 8 + HEADS + head : 9 + HEADS + head]
        cumul_row = sums[HEADS + head : HEADS + head + 1]
        last = cumul[CHUNK - 1 :]
        decays = jnp.where(
            rows >= cols, jnp.exp(jnp.minimum(cumul - cumul_row, 0.0)), 0.0
        )
        strict = jnp.where(rows > cols, dots[:CHUNK] * decays * beta, 0.0)
        inverse = lower_inverse(strict, rows, cols)
        grown = jnp.exp(cumul)
        right = jnp.concatenate(
            [values[:, head * DV : (head + 1) * DV] * beta, keys * (beta * grown)], 1
        )
        solved = mm(inverse, right)
        key_tail = keys * jnp.exp(last - cumul)
        mixing = dots[CHUNK:] * decays
        both = mm(jnp.concatenate([key_tail.T, mixing], 0), solved)
        move = jnp.concatenate([-both[:DK, DV:], queries * grown - both[DK:, DV:]], 0)
        move_ref[block, head] = move.astype(BF)
        add_ref[block, head] = both[:, :DV]
        tail_ref[block, head] = jnp.broadcast_to(jnp.exp(last), (8, DV))


def run_states(start, move_ref, add_ref, tail_ref, z_ref, gain, length, store):
    states = [start[head] for head in range(HEADS)]
    for block in range(BLOCKS):
        place = block * CHUNK + lax.broadcasted_iota(jnp.int32, (CHUNK, 1), 0)
        valid = (place < length).astype(F32)
        for head in range(HEADS):
            result = mm(move_ref[block, head], states[head]) + add_ref[block, head]
            states[head] = tail_ref[block, head][0:1] * states[head] + result[:DK]
            out = result[DK:]
            scale = lax.rsqrt(jnp.mean(out * out, -1, keepdims=True) + EPS)
            gate = z_ref[pl.ds(block * CHUNK + PAD, CHUNK), head * DV : (head + 1) * DV]
            store(block, head, (out * scale * gain * silu(gate) * valid).astype(BF))
    return states


def mixer_kernel(
    q_in, k_in, v_in, z_in, raw, taps, a_log, dt_bias, lengths, gain, start,
    mixed, final, q_ref, k_ref, v_ref, z_ref, move_ref, add_ref, tail_ref,
):
    request = pl.program_id(0)
    length = lengths[request]
    for source, target in ((q_in, q_ref), (k_in, k_ref), (v_in, v_ref), (z_in, z_ref)):
        target[0:PAD] = jnp.zeros((PAD, target.shape[1]), F32)
        target[PAD:] = source[...]
    gates = gate_rows(raw[...], a_log, dt_bias, length)
    tap_rows = taps[...]
    for block in range(BLOCKS):
        block_terms(
            block, q_ref, k_ref, v_ref, tap_rows,
            gates[:, block * CHUNK : (block + 1) * CHUNK], move_ref, add_ref, tail_ref,
        )

    def store(block, head, rows):
        mixed[pl.ds(block * CHUNK, CHUNK), head * DV : (head + 1) * DV] = rows

    states = run_states(
        [start[0, head] for head in range(HEADS)],
        move_ref, add_ref, tail_ref, z_ref, gain[...], length, store,
    )
    for head in range(HEADS):
        final[0, head] = states[head]


def mixer(q, k, v, z, raw, taps, a_log, dt_bias, lengths, gain, start):
    requests = lengths.shape[0]
    smem = pl.BlockSpec(memory_space=pltpu.SMEM)

    def rows(width):
        return pl.BlockSpec((SUF, width), lambda r: (r, 0))

    return pl.pallas_call(
        mixer_kernel,
        grid=(requests,),
        in_specs=[
            rows(DK), rows(DK), rows(HEADS * DV), rows(HEADS * DV),
            pl.BlockSpec((2 * HEADS, SUF), lambda r: (0, r)),
            pl.BlockSpec((CONV, 2 * DK + HEADS * DV), lambda r: (0, 0)),
            smem, smem, smem,
            pl.BlockSpec((1, DV), lambda r: (0, 0)),
            pl.BlockSpec((1, HEADS, DK, DV), lambda r: (r, 0, 0, 0)),
        ],
        out_specs=[
            rows(HEADS * DV),
            pl.BlockSpec((1, HEADS, DK, DV), lambda r: (r, 0, 0, 0)),
        ],
        out_shape=[
            jax.ShapeDtypeStruct((requests * SUF, HEADS * DV), BF),
            jax.ShapeDtypeStruct((requests, HEADS, DK, DV), F32),
        ],
        scratch_shapes=[
            pltpu.VMEM((PAD + SUF, DK), F32),
            pltpu.VMEM((PAD + SUF, DK), F32),
            pltpu.VMEM((PAD + SUF, HEADS * DV), F32),
            pltpu.VMEM((PAD + SUF, HEADS * DV), F32),
            pltpu.VMEM((BLOCKS, HEADS, 2 * CHUNK, DK), BF),
            pltpu.VMEM((BLOCKS, HEADS, 2 * CHUNK, DV), F32),
            pltpu.VMEM((BLOCKS, HEADS, 8, DV), F32),
        ],
        compiler_params=pltpu.CompilerParams(vmem_limit_bytes=48 * 1024 * 1024),
        cost_estimate=pl.CostEstimate(flops=2 * 10**9, bytes_accessed=8 * 10**6, transcendentals=10**6),
    )(q, k, v, z, raw, taps, a_log, dt_bias, lengths, gain, start)


def normalize(token_rows, gain):
    floats = token_rows.astype(F32)
    return floats * lax.rsqrt(jnp.mean(floats * floats, -1, keepdims=True) + EPS) * gain


def on_device(
    tokens, in_gain, w_query, w_key, w_value, w_gate_z, w_beta, w_decay,
    conv_query, conv_key, conv_value, a_log, dt_bias, out_gain, w_out,
    state_pool, hit_owner, hit_slot, lengths,
):
    requests = lengths.shape[0]
    head_count = state_pool.shape[1]
    wanted = (hit_owner * SLOTS + hit_slot).reshape(-1)
    piece = lax.all_gather(state_pool.astype(BF), "req", axis=0, tiled=True)
    starts = piece[wanted].astype(F32).reshape(requests, L, head_count, DK, DV)

    def dot(a, b):
        return jnp.dot(a, b, preferred_element_type=F32)

    def branch(rows_in, level):
        normed = normalize(rows_in, in_gain[level]).astype(BF)
        everyone = lax.all_gather(normed, "head", axis=0, tiled=True)
        small = jnp.concatenate([w_beta[level], w_decay[level]], 1)
        raw = lax.dot_general(small, everyone, (((0,), (1,)), ((), ())), preferred_element_type=F32)
        taps = jnp.concatenate([conv_query[level], conv_key[level], conv_value[level]], 1)
        mixed, final = mixer(
            dot(everyone, w_query[level]), dot(everyone, w_key[level]),
            dot(everyone, w_value[level]), dot(everyone, w_gate_z[level]),
            raw, taps, a_log[level], dt_bias[level], lengths, out_gain[level : level + 1],
            starts[:, level],
        )
        added = lax.psum_scatter(
            dot(mixed, w_out[level]).astype(BF), "head", scatter_dimension=0, tiled=True
        ).astype(F32)
        return (rows_in.astype(F32) + added).astype(BF), final

    current, first_end = branch(tokens, 0)
    result, second_end = branch(current, 1)
    return (result, jnp.stack([first_end, second_end], 1))


def solution(mesh):
    heads = P(None, None, "head")
    in_specs = (
        P(("req", "head"), None), P(), heads, heads, heads, heads, heads, heads,
        heads, heads, heads, P(None, "head"), P(None, "head"), P(),
        P(None, "head", None), P("req", "head", None, None),
        P("req", None), P("req", None), P("req"),
    )
    out_specs = (P(("req", "head"), None), P("req", None, "head", None, None))
    return jax.shard_map(
        on_device, mesh=mesh, in_specs=in_specs, out_specs=out_specs, check_vma=False
    )
```

time: 470 us -> 367 us (0.78); the launches traced: 462 us -> 366 us
  matrix products: 147 us -> 23.5 us
  Pallas kernels: 0 us -> 55.1 us
  local copies, waits for them, and re-layouts: 24.7 us -> 9.25 us
  other arithmetic: 24.8 us -> 10.2 us
    dot_general x105 -> x12, matrix products: 147 us -> 23.5 us  [the longest x10 21.2 us: dot(): return jnp.dot(a, b, preferred_element_type=F32)]
    pallas_call x0 -> x2, Pallas kernels: none -> 55.1 us  [mixer(): pl.pallas_call(mixer_kernel, grid=(requests,), in_specs=[rows(DK), rows(D...]
    mul x10 -> x0, other arithmetic: 6.99 us -> none  [the longest x2 3.3 us: mixer(): jax.nn.silu(causal_conv(pieces[2], kernels[2]))]
    transpose x12 -> x0, local copies, waits for them, and re-layouts: 6.56 us -> none  [the longest x4 3.38 us: delta_blocks(): jnp.moveaxis(array, 1, 0)]
    dot_general x3 -> x0, local copies, waits for them, and re-layouts: 5.54 us -> none  [project(): jnp.dot(normed, weight, preferred_element_type=jnp.float32)]
    reshape x2 -> x1, local copies, waits for them, and re-layouts: 5.53 us -> 0.08 us  [on_device(): wanted = (hit_owner * SLOTS + hit_slot).reshape(-1)]
where the time goes in v1:
time: 367 us; the launch traced here: 366 us
  waiting for transfers between devices  253 us (69%)
  Pallas kernels  55.1 us (15%)
  matrix products  23.5 us (6%)
  between operations  14 us (4%)
  other arithmetic  10.2 us (3%)
  local copies, waits for them, and re-layouts  9.25 us (3%)
    reduce_scatter x2, waiting for transfers between devices, branch(): lax.psum_scatter(dot(mixed, w_out[level]).astype(BF), 'head', scatter_dim...  132 us
    all_gather x2, waiting for transfers between devices, branch(): everyone = lax.all_gather(normed, 'head', axis=0, tiled=True)  72.1 us
    pallas_call x2, Pallas kernels, mixer(): pl.pallas_call(mixer_kernel, grid=(requests,), in_specs=[rows(DK), rows(D...  55.1 us
    all_gather x1, waiting for transfers between devices, on_device(): piece = lax.all_gather(state_pool.astype(BF), 'req', axis=0, tiled=True)  49.1 us
    dot_general x10, matrix products, dot(): return jnp.dot(a, b, preferred_element_type=F32)  21.2 us
  transfers between devices with their start and end apart: 5, of which 5 were waited for; matrix products, arithmetic and copies ran while one was open for 3% of the time, Pallas kernels for 0%

profile of v1, /device:TPU:2, one launch (start us, length us, event | category | flops | bytes accessed | tf_op | source)
XLA Modules:
  0.0 365.6 jit_solution(15108397694923011287)
XLA Ops:
  7.2 0.0 copy-start.10
  7.2 0.0 all-gather.6.cloned.1.call-start
  7.2 1.9 convert_element_type.44
  9.1 0.0 all-gather.6.cloned.1.call-update
  9.1 0.0 all-gather.4.cloned.1.call-start
  9.2 1.1 fusion.16
  10.3 0.8 fusion.47
  11.1 1.8 fusion.18
  12.9 0.0 all-gather.4.cloned.1.call-update
  12.9 0.0 reduce-scatter.3.cloned.1.call-start
  13.0 0.7 multiply_add_fusion
  13.7 0.1 reshape.55
  13.8 0.7 slice_bitcast_fusion.6
  14.5 0.7 slice_bitcast_fusion.8
  15.2 0.8 fusion.48
  16.0 0.8 slice_bitcast_fusion.12
  16.7 0.8 slice_bitcast_fusion.2
  17.5 49.1 %all-gather.6.cloned.1.call-done = bf16[32,2,128,128]{3,2,1,0:T(8,128)(2,1)} async-done(((bf16[4,2,128,128]{3,2,1,0:T(8,128)(2,1)}), bf16[32,2,128,128]{3,2,1,0:T(8,128)(2,1)}) %all-gather.6.cloned.1.call-update) | async-done | bytes 2097168 | tf_op jit(solution)/shard_map/all_gather | solution.py:215
  66.6 2.2 gather_fusion
  68.8 0.0 copy-start.11
  68.9 35.7 %all-gather.4.cloned.1.call-done = bf16[1024,2048]{1,0:T(8,128)(2,1)} async-done(((bf16[64,2048]{1,0:T(8,128)(2,1)}), bf16[1024,2048]{1,0:T(8,128)(2,1)}) %all-gather.4.cloned.1.call-update) | async-done | bytes 4194320 | tf_op jit(solution)/shard_map/all_gather | solution.py:223
  104.6 0.0 copy-done.10
  104.6 0.0 copy-start.2
  104.6 3.6 fusion.28.k_in
  108.2 0.0 copy-done.11
  108.2 0.0 copy-done.2
  108.2 0.0 copy-start.6
  108.2 1.2 fusion.30.q_in
  109.5 0.3 copy-done.6
  109.8 1.3 fusion.6.z_in
  111.1 0.3 copy-done.8
  111.4 1.2 fusion.8.v_in
  112.7 1.2 fusion.36.raw
  113.9 0.0 copy-done
  113.9 27.5 %shard_map.194 = (bf16[1024,256]{1,0:T(8,128)(2,1)S(1)}, f32[2,2,128,128]{3,2,1,0:T(8,128)S(1)}) custom-call(f32[1024,128]{1,0:T(8,128)S(1)} %fusion.30.q_in, f32[1024,128]{1,0:T(8,128)S(1)} %fusion.28.k_in, f32[1024,256]{1,0:T(8,128)S(1)} %fusion.8.v_in, f32[1024,256]{1,0:T(8,128)S(1)} %fusion.6.z_in, f32[4,1024]{1,0:T(4,128)S(1)} %fusion.36.raw, ...), custom_call_target="tpu_custom_call" | custom-call | flops 2000000000 | bytes 8000000 | tf_op jit(solution)/shard_map/pallas_call | solution.py:169
  141.4 0.0 copy-done.5
  141.4 0.0 copy-start.1
  141.4 3.2 convolution_convert_fusion.1
  144.6 0.0 reduce-scatter.3.cloned.1.call-update
  144.7 0.0 all-gather.8.cloned.1.call-start
  144.7 66.4 %reduce-scatter.3.cloned.1.call-done = bf16[64,2048]{1,0:T(8,128)(2,1)} async-done(((bf16[1024,2048]{1,0:T(8,128)(2,1)}), bf16[64,2048]{1,0:T(8,128)(2,1)}) %reduce-scatter.3.cloned.1.call-update) | async-done | bytes 262160 | tf_op jit(solution)/shard_map/reduce_scatter | solution.py:233
  211.1 0.0 copy-done.1
  211.1 1.1 fusion.20
  212.2 1.8 fusion.22
  214.0 0.0 all-gather.8.cloned.1.call-update
  214.0 0.3 reduce-scatter.5.cloned.1.call-start
  214.3 36.4 %all-gather.8.cloned.1.call-done = bf16[1024,2048]{1,0:T(8,128)(2,1)} async-done(((bf16[64,2048]{1,0:T(8,128)(2,1)}), bf16[1024,2048]{1,0:T(8,128)(2,1)}) %all-gather.8.cloned.1.call-update) | async-done | bytes 4194320 | tf_op jit(solution)/shard_map/all_gather | solution.py:223
  250.7 3.7 %fusion.24.k_in = f32[1024,128]{1,0:T(8,128)S(1)} fusion(bf16[1024,2048]{1,0:T(8,128)(2,1)} %all-gather.8.cloned.1.call-done, bf16[2,2048,128]{2,1,0:T(8,128)(2,1)} %param.22), kind=kOutput, calls=%fused_computation.34 | convolution fusion | flops 536870912 | bytes 5242880 | tf_op jit(solution)/shard_map/dot_general | solution.py:219
  254.4 0.0 copy-done.3
  254.4 0.2 copy-done.12
  254.6 1.2 fusion.26.q_in
  255.8 0.3 copy-done.7
  256.2 1.2 fusion.1.z_in
  257.4 0.3 copy-done.9
  257.8 1.3 fusion.3.v_in
  259.0 1.2 fusion.40.raw
  260.2 27.6 %shard_map.195 = (bf16[1024,256]{1,0:T(8,128)(2,1)S(1)}, f32[2,2,128,128]{3,2,1,0:T(8,128)S(1)}) custom-call(f32[1024,128]{1,0:T(8,128)S(1)} %fusion.26.q_in, f32[1024,128]{1,0:T(8,128)S(1)} %fusion.24.k_in, f32[1024,256]{1,0:T(8,128)S(1)} %fusion.3.v_in, f32[1024,256]{1,0:T(8,128)S(1)} %fusion.1.z_in, f32[4,1024]{1,0:T(4,128)S(1)} %fusion.40.raw, ...), custom_call_target="tpu_custom_call" | custom-call | flops 2000000000 | bytes 8000000 | tf_op jit(solution)/shard_map/pallas_call | solution.py:169
  287.8 3.2 convolution_convert_fusion
  291.0 0.0 reduce-scatter.5.cloned.1.call-update
  291.0 0.1 pad_maximum_fusion
  291.1 0.8 copy.27
  291.9 65.4 %reduce-scatter.5.cloned.1.call-done = bf16[64,2048]{1,0:T(8,128)(2,1)} async-done(((bf16[1024,2048]{1,0:T(8,128)(2,1)}), bf16[64,2048]{1,0:T(8,128)(2,1)}) %reduce-scatter.5.cloned.1.call-update) | async-done | bytes 262160 | tf_op jit(solution)/shard_map/reduce_scatter | solution.py:233
  357.3 0.0 copy-done.4
  357.3 1.8 fusion.23
  (16 shorter events, 0.1 us)
Async XLA Ops:
  7.2 97.5 %copy-start.10 = (bf16[2,2048,128]{2,1,0:T(8,128)(2,1)S(1)}, bf16[2,2048,128]{2,1,0:T(8,128)(2,1)}, u32[]{:S(2)}) copy-start(bf16[2,2048,128]{2,1,0:T(8,128)(2,1)} %param.22) | copy-start | bytes 3145732
  7.2 59.4 %all-gather.6.cloned.1.call-start = ((), (), s32[]{:S(2)}) async-start(), calls=%async_computation.3 | async-start | bytes 2359296 | tf_op jit(solution)/shard_map/all_gather | solution.py:215
  9.1 95.5 %all-gather.4.cloned.1.call-start = ((), (), s32[]{:S(2)}) async-start(), calls=%async_computation.2 | async-start | bytes 4456448 | tf_op jit(solution)/shard_map/all_gather | solution.py:223
  12.9 198.2 %reduce-scatter.3.cloned.1.call-start = ((), (), s32[]{:S(2)}) async-start(), calls=%async_computation.4 | async-start | bytes 4456448 | tf_op jit(solution)/shard_map/reduce_scatter | solution.py:233
  68.8 39.4 %copy-start.11 = (bf16[2,2048,128]{2,1,0:T(8,128)(2,1)S(1)}, bf16[2,2048,128]{2,1,0:T(8,128)(2,1)}, u32[]{:S(2)}) copy-start(bf16[2,2048,128]{2,1,0:T(8,128)(2,1)} %param.21) | copy-start | bytes 3145732
  104.6 3.6 copy-start.2
  108.2 1.6 copy-start.6
  109.8 1.6 copy-start.8
  111.4 2.4 copy-start
  113.9 27.5 %copy-start.5 = (bf16[2,256,2048]{2,1,0:T(8,128)(2,1)S(1)}, bf16[2,256,2048]{2,1,0:T(8,128)(2,1)}, u32[]{:S(2)}) copy-start(bf16[2,256,2048]{2,1,0:T(8,128)(2,1)} %param.33) | copy-start | bytes 6291460
  141.4 69.7 %copy-start.1 = (bf16[64,2048]{1,0:T(8,128)(2,1)S(1)}, bf16[64,2048]{1,0:T(8,128)(2,1)}, u32[]{:S(2)}) copy-start(bf16[64,2048]{1,0:T(8,128)(2,1)} %param.19) | copy-start | bytes 786436
  144.7 106.0 %all-gather.8.cloned.1.call-start = ((), (), s32[]{:S(2)}) async-start(), calls=%async_computation.5 | async-start | bytes 4456448 | tf_op jit(solution)/shard_map/all_gather | solution.py:223
  214.0 143.2 %reduce-scatter.5.cloned.1.call-start = ((), (), s32[]{:S(2)}) async-start(), calls=%async_computation.6 | async-start | bytes 4456448 | tf_op jit(solution)/shard_map/reduce_scatter | solution.py:233
  250.7 3.7 %copy-start.3 = (bf16[1024,2048]{1,0:T(8,128)(2,1)S(1)}, bf16[1024,2048]{1,0:T(8,128)(2,1)}, u32[]{:S(2)}) copy-start(bf16[1024,2048]{1,0:T(8,128)(2,1)} %all-gather.8.cloned.1.call-done) | copy-start | bytes 12582916
  250.7 3.9 %copy-start.12 = (bf16[2,2048,128]{2,1,0:T(8,128)(2,1)S(1)}, bf16[2,2048,128]{2,1,0:T(8,128)(2,1)}, u32[]{:S(2)}) copy-start(bf16[2,2048,128]{2,1,0:T(8,128)(2,1)} %param.21) | copy-start | bytes 3145732
  254.6 1.6 copy-start.7
  256.2 1.6 copy-start.9
  291.0 66.3 %copy-start.4 = (bf16[64,2048]{1,0:T(8,128)(2,1)S(1)}, bf16[64,2048]{1,0:T(8,128)(2,1)}, u32[]{:S(2)}) copy-start(bf16[64,2048]{1,0:T(8,128)(2,1)} %reduce-scatter.3.cloned.1.call-done) | copy-start | bytes 786436
Sparse Core Ops, SparseCore 0:
  10.9 55.5 all-gather.5
  68.8 35.7 all-gather.3
  144.8 66.2 reduce-scatter.2
  214.2 36.4 all-gather.7
  291.1 66.0 reduce-scatter.4

commit v2 on v1

v2 whole, which is shorter than its diff:
```python
import jax
import jax.numpy as jnp
from jax import lax
from jax.experimental import pallas as pl
from jax.experimental.pallas import tpu as pltpu
from jax.sharding import PartitionSpec as P

DK = 128
DV = 128
L = 2
SLOTS = 4
SUF = 512
CONV = 4
HEADS = 2
CHUNK = 128
BLOCKS = SUF // CHUNK
PAD = 8
EPS = 1e-06
BF = jnp.bfloat16
F32 = jnp.float32
D = 2048
ROWS = 64
PIECE = 16
PIECES = ROWS // PIECE
WIDE = 2 * DK + 2 * HEADS * DV
SEMS = 176


def silu(v):
    return v / (1.0 + jnp.exp(-v))


def conv_block(ref, row, width, taps):
    window = ref[pl.ds(row, CHUNK + PAD), 0:width]
    total = None
    for tap in range(CONV):
        first = PAD - (CONV - 1) + tap
        term = window[first : first + CHUNK] * taps[tap : tap + 1]
        total = term if total is None else total + term
    return silu(total)


def unit_rows(vectors):
    return vectors * lax.rsqrt(jnp.sum(vectors * vectors, -1, keepdims=True) + EPS)


def mm(a, b):
    return jnp.dot(a.astype(BF), b.astype(BF), preferred_element_type=F32)


def nt(a, b):
    return lax.dot_general(
        a.astype(BF), b.astype(BF), (((1,), (1,)), ((), ())), preferred_element_type=F32
    )


def lower_inverses(stricts, rows, cols):
    size = 16
    near = rows // size == cols // size
    eye = jnp.where(rows == cols, 1.0, 0.0)
    diags = [jnp.where(near, -strict, 0.0) for strict in stricts]
    inverses = [eye + diag for diag in diags]
    powers = [mm(diag, diag) for diag in diags]
    for _ in range(2):
        both = [
            mm(jnp.concatenate([power, inverse], 0), power)
            for power, inverse in zip(powers, inverses)
        ]
        inverses = [inverse + pair[CHUNK:] for inverse, pair in zip(inverses, both)]
        powers = [pair[:CHUNK] for pair in both]
    inverses = [inverse + mm(inverse, power) for inverse, power in zip(inverses, powers)]
    while size < CHUNK:
        joined = (rows // (2 * size) == cols // (2 * size)) & (rows // size > cols // size)
        halves = [
            mm(jnp.where(joined, strict, 0.0), inverse)
            for strict, inverse in zip(stricts, inverses)
        ]
        inverses = [inverse - mm(inverse, half) for inverse, half in zip(inverses, halves)]
        size *= 2
    return inverses


def gate_rows(raw, a_log, dt_bias, valid):
    rows = []
    for head in range(HEADS):
        rows.append(jnp.where(valid, 1.0 / (1.0 + jnp.exp(-raw[head : head + 1])), 0.0))
    for head in range(HEADS):
        shifted = raw[HEADS + head : HEADS + head + 1] + dt_bias[head]
        soft = jnp.maximum(shifted, 0.0) + jnp.log1p(jnp.exp(-jnp.abs(shifted)))
        rate = jnp.exp(jnp.full((1, CHUNK), a_log[head], F32))
        rows.append(jnp.where(valid, -rate * soft, 0.0))
    rows.append(jnp.zeros((8 - 2 * HEADS, CHUNK), F32))
    return jnp.concatenate(rows, 0)


def block_terms(blocks, q_ref, k_ref, v_ref, raws, taps, a_log, dt_bias, length, move_ref, add_ref, tail_ref):
    rows = lax.broadcasted_iota(jnp.int32, (CHUNK, CHUNK), 0)
    cols = lax.broadcasted_iota(jnp.int32, (CHUNK, CHUNK), 1)
    lane = lax.broadcasted_iota(jnp.int32, (1, CHUNK), 1)
    upper = jnp.where(rows <= cols, 1.0, 0.0)
    gates = [
        gate_rows(raw, a_log, dt_bias, block * CHUNK + lane < length)
        for block, raw in zip(blocks, raws)
    ]
    sums = jnp.dot(
        jnp.concatenate(gates, 0), upper, precision=lax.Precision.HIGHEST, preferred_element_type=F32
    )
    sums = [sums[8 * index : 8 * index + 8] for index in range(len(blocks))]
    columns = [jnp.concatenate([gate, total], 0).T for gate, total in zip(gates, sums)]
    keys = [unit_rows(conv_block(k_ref, block * CHUNK, DK, taps[1])) for block in blocks]
    queries = [
        unit_rows(conv_block(q_ref, block * CHUNK, DK, taps[0])) * DK ** (-0.5) for block in blocks
    ]
    dots = [nt(jnp.concatenate([key, query], 0), key) for key, query in zip(keys, queries)]
    units = [(index, head) for index in range(len(blocks)) for head in range(HEADS)]
    stricts, decays = [], []
    for index, head in units:
        cumul = columns[index][:, 8 + HEADS + head : 9 + HEADS + head]
        cumul_row = sums[index][HEADS + head : HEADS + head + 1]
        decay = jnp.where(rows >= cols, jnp.exp(jnp.minimum(cumul - cumul_row, 0.0)), 0.0)
        beta = columns[index][:, head : head + 1]
        stricts.append(jnp.where(rows > cols, dots[index][:CHUNK] * decay * beta, 0.0))
        decays.append(decay)
    inverses = lower_inverses(stricts, rows, cols)
    values = [conv_block(v_ref, block * CHUNK, HEADS * DV, taps[2]) for block in blocks]
    solved = []
    for (index, head), inverse in zip(units, inverses):
        beta = columns[index][:, head : head + 1]
        grown = jnp.exp(columns[index][:, 8 + HEADS + head : 9 + HEADS + head])
        right = jnp.concatenate(
            [values[index][:, head * DV : (head + 1) * DV] * beta, keys[index] * (beta * grown)], 1
        )
        solved.append(mm(inverse, right))
    for (index, head), decay, solution_now in zip(units, decays, solved):
        cumul = columns[index][:, 8 + HEADS + head : 9 + HEADS + head]
        last = cumul[CHUNK - 1 :]
        key_tail = keys[index] * jnp.exp(last - cumul)
        mixing = dots[index][CHUNK:] * decay
        both = mm(jnp.concatenate([key_tail.T, mixing], 0), solution_now)
        move = jnp.concatenate(
            [-both[:DK, DV:], queries[index] * jnp.exp(cumul) - both[DK:, DV:]], 0
        )
        move_ref[blocks[index], head] = move.astype(BF)
        add_ref[blocks[index], head] = both[:, :DV]
        tail_ref[blocks[index], head] = jnp.broadcast_to(jnp.exp(last), (8, DV))


def run_states(start, move_ref, add_ref, tail_ref, z_ref, gain, length, store):
    states = [start[head] for head in range(HEADS)]
    for block in range(BLOCKS):
        place = block * CHUNK + lax.broadcasted_iota(jnp.int32, (CHUNK, 1), 0)
        valid = (place < length).astype(F32)
        results = [
            mm(move_ref[block, head], states[head]) + add_ref[block, head] for head in range(HEADS)
        ]
        for head in range(HEADS):
            states[head] = tail_ref[block, head][0:1] * states[head] + results[head][:DK]
            out = results[head][DK:]
            scale = lax.rsqrt(jnp.mean(out * out, -1, keepdims=True) + EPS)
            gate = z_ref[pl.ds(block * CHUNK, CHUNK), head * DV : (head + 1) * DV]
            store(block, head, (out * scale * gain * silu(gate) * valid).astype(BF))
    return states


def spot(x, y, core):
    return x * 8 + y * 2 + core


def piece(index):
    return pl.ds(index * PIECE, PIECE)


def layers_kernel(
    tokens, in_gain, w_query, w_key, w_value, w_gate, w_beta, w_decay,
    conv_query, conv_key, conv_value, a_log, dt_bias, out_gain, w_out,
    pool, owner, slot, lengths, wanted,
    out_rows, final,
    weights, outs, buf, q_ref, k_ref, v_ref, z_ref, raw_ref, move_ref, add_ref, tail_ref,
    mixed, stage, sib, land, last_land, held, current, pool_in, zbuf, xsend, xland,
    table_in, table, send_sems, recv_sems, local_sems,
):
    me = lax.axis_index("head")
    group = lax.axis_index("req")
    x, y, core = me // 8, (me // 2) % 4, me % 2
    z, high = group // 2, group % 2
    other, up, down, far = 1 - x, (y + 1) % 4, (y + 3) % 4, (y + 2) % 4

    def plane(a, b):
        return spot(a, b, core)

    to_x, to_up, to_down = ({"head": plane(other, y)}, {"head": plane(x, up)}, {"head": plane(x, down)})
    sibling = {"head": spot(x, y, 1 - core)}
    to_high = {"req": z * 2 + 1 - high}
    to_z = [{"req": ((z + step) % 4) * 2 + high} for step in (1, 3, 2)]

    copies = []

    def send(source, target, device):
        index = len(copies)
        copy = pltpu.make_async_remote_copy(
            src_ref=source,
            dst_ref=target,
            send_sem=send_sems.at[index],
            recv_sem=recv_sems.at[index],
            device_id=device,
            device_id_type=pl.DeviceIdType.MESH,
        )
        copy.start()
        copies.append(copy)
        return copy

    loads = []

    def load(source, target):
        copy = pltpu.make_async_copy(source, target, local_sems.at[len(loads)])
        copy.start()
        loads.append(copy)
        return copy

    pool_load = load(pool, pool_in)
    weight_loads, out_loads = [], []
    for level in range(L):
        first = 0
        mine = []
        for source, width in (
            (w_query, DK), (w_key, DK), (w_value, HEADS * DV), (w_gate, HEADS * DV),
        ):
            mine.append(
                load(source.at[level], weights.at[level, :, pl.ds(first, width)])
            )
            first += width
        weight_loads.append(mine)
        out_loads.append(load(w_out.at[level], outs.at[level]))

    barrier = pltpu.get_barrier_semaphore()
    partners = [to_x, to_up, to_down, sibling, to_high] + to_z
    for partner in partners:
        pl.semaphore_signal(
            barrier, inc=1, device_id=partner, device_id_type=pl.DeviceIdType.MESH
        )
    pl.semaphore_wait(barrier, len(partners))

    current[...] = tokens[...]
    for ref in (q_ref, k_ref, v_ref):
        ref[:, 0:PAD] = jnp.zeros((2, PAD, ref.shape[2]), F32)

    def small_weights(level):
        rows = jnp.concatenate(
            [
                w_beta[level].astype(F32),
                w_decay[level].astype(F32),
                jnp.zeros((128 - 2 * HEADS, D), F32),
            ],
            0,
        )
        weights[level, :, WIDE:] = rows.T.astype(BF)

    def gather_start(level):
        floats = current[...].astype(F32)
        scale = lax.rsqrt(jnp.mean(floats * floats, -1, keepdims=True) + EPS)
        buf[level, me] = (floats * scale * in_gain[level : level + 1]).astype(BF)
        parts = {"x1": [], "p1": [], "m1": []}
        for p in range(PIECES):
            ref = buf.at[level, me, piece(p)]
            parts["p1"].append(send(ref, ref, to_up))
            parts["m1"].append(send(ref, ref, to_down))
            parts["x1"].append(send(ref, ref, to_x))
        parts["own"] = send(buf.at[level, me], buf.at[level, me], sibling)
        return parts

    def pass_block(level, block, rows=None):
        ref = buf.at[level, block] if rows is None else buf.at[level, block, rows]
        return send(ref, ref, sibling)

    def pass_piece(level, block, p, device):
        ref = buf.at[level, block, piece(p)]
        return send(ref, ref, device)

    def gather_near(level, parts):
        parts["p2"], parts["m2"], parts["p3"], parts["m3"] = [], [], [], []
        for p in range(PIECES):
            parts["p1"][p].wait_recv()
            if p < PIECES // 2:
                parts["p2"].append(pass_piece(level, plane(x, down), p, to_up))
            parts["m1"][p].wait_recv()
            if p >= PIECES // 2:
                parts["m2"].append(pass_piece(level, plane(x, up), p, to_down))
            parts["x1"][p].wait_recv()
            parts["p3"].append(pass_piece(level, plane(other, y), p, to_up))
            parts["m3"].append(pass_piece(level, plane(other, y), p, to_down))
        parts["down"] = pass_block(level, plane(x, down))
        parts["up"] = pass_block(level, plane(x, up))
        parts["across"] = pass_block(level, plane(other, y))

    def gather_far(level, parts):
        half = PIECES // 2
        parts["x2"] = []
        block = plane(x, far)
        for p in range(half):
            parts["p2"][p].wait_recv()
            parts["x2"].append(pass_piece(level, block, p, to_x))
        parts["far1"] = pass_block(level, block, pl.ds(0, ROWS // 2))
        for p in range(half):
            parts["m2"][p].wait_recv()
            parts["x2"].append(pass_piece(level, block, half + p, to_x))
        parts["far2"] = pass_block(level, block, pl.ds(ROWS // 2, ROWS // 2))

    def gather_rest(level, parts):
        for name, place in (("p3", down), ("m3", up), ("x2", far)):
            for copy in parts[name]:
                copy.wait_recv()
            parts[name + "s"] = pass_block(level, plane(other, place))

    def keep(level, request, result, row, count):
        place = pl.ds(row + PAD, count)
        q_ref[request, place] = result[:, 0:DK]
        k_ref[request, place] = result[:, DK : 2 * DK]
        v_ref[request, place] = result[:, 2 * DK : 2 * DK + HEADS * DV]
        z_ref[request, pl.ds(row, count)] = result[:, 2 * DK + HEADS * DV : WIDE]
        raw_ref[request, pl.ds(row, count)] = result[:, WIDE:]

    def project_chunk(level, b):
        rows = buf[level, pl.ds(spot(x, b, 0), 2)].reshape(CHUNK, D)
        result = jnp.dot(rows, weights[level], preferred_element_type=F32)
        keep(level, x, result, pl.multiple_of(b * CHUNK, CHUNK), CHUNK)

    def project_request(level, request):
        rows = buf[level, pl.ds(request * 8, 8)].reshape(SUF, D)
        result = jnp.dot(rows, weights[level], preferred_element_type=F32)
        keep(level, request, result, 0, SUF)

    def mix_blocks(level, request):
        blocks = list(range(BLOCKS))
        raws = [
            raw_ref[request, pl.ds(block * CHUNK, CHUNK)].T[0 : 2 * HEADS] for block in blocks
        ]
        block_terms(
            blocks, q_ref.at[request], k_ref.at[request], v_ref.at[request], raws,
            (conv_query[level], conv_key[level], conv_value[level]),
            [a_log[level, head] for head in range(HEADS)],
            [dt_bias[level, head] for head in range(HEADS)],
            lengths[request], move_ref, add_ref, tail_ref,
        )

    def mix_states(level, request):
        holder = owner[request, level]
        near = zbuf[(holder // 2) * SLOTS + slot[request, level]]
        start = jnp.where(holder % 2 == high, near, xland[request * L + level]).astype(F32)

        def store(block, head, rows):
            mixed[pl.ds(block * CHUNK, CHUNK), head * DV : (head + 1) * DV] = rows

        states = run_states(
            start, move_ref, add_ref, tail_ref, z_ref.at[request], out_gain[level : level + 1],
            lengths[request], store,
        )
        for head in range(HEADS):
            final[request, level, head] = states[head]

    def kept(level, half, index, p):
        row = pl.multiple_of(core * ROWS + p * PIECE, PIECE)
        mine = stage[level, half, index, pl.ds(row, PIECE)].astype(F32)
        return mine + sib[level, half, index, piece(p)].astype(F32)

    def scatter_start(level, half):
        pairs = []
        for index, b in enumerate((far, down, up, y)):
            rows = mixed[pl.ds(pl.multiple_of(b * CHUNK, CHUNK), CHUNK)]
            stage[level, half, index] = jnp.dot(
                rows, outs[level], preferred_element_type=F32
            ).astype(BF)
            theirs = pl.ds(pl.multiple_of((1 - core) * ROWS, ROWS), ROWS)
            pairs.append(send(stage.at[level, half, index, theirs], sib.at[level, half, index], sibling))
        middle = PIECES // 2
        todo = {"pairs": pairs, "b": [None] * PIECES, "cd": [None] * PIECES, "cu": [None] * PIECES}

        def pass_on(index, p, device, name, where):
            sib[level, half, index, piece(p)] = kept(level, half, index, p).astype(BF)
            todo[name][p] = send(
                sib.at[level, half, index, piece(p)], land.at[level, half, where, piece(p)], device
            )

        pairs[0].wait_recv()
        for p in range(middle):
            pass_on(0, p, to_down, "b", 0)
            pass_on(0, p + middle, to_up, "b", 0)
        pairs[1].wait_recv()
        for p in range(middle, PIECES):
            pass_on(1, p, to_down, "cd", 1)
        pairs[2].wait_recv()
        for p in range(middle):
            pass_on(2, p, to_up, "cu", 2)
        pairs[3].wait_recv()
        return todo

    def scatter_middle(level, half, todo):
        middle = PIECES // 2
        for step in range(middle):
            for p, index, device, name in (
                (step, 1, to_down, "cd"), (step + middle, 2, to_up, "cu"),
            ):
                todo["b"][p].wait_recv()
                total = kept(level, half, index, p) + land[level, half, 0, piece(p)].astype(F32)
                sib[level, half, index, piece(p)] = total.astype(BF)
                todo[name][p] = send(
                    sib.at[level, half, index, piece(p)], land.at[level, half, index, piece(p)], device
                )

    def scatter_end(level, half, todo, use):
        middle = PIECES // 2
        for step in range(middle):
            for p in (step, step + middle):
                todo["cd"][p].wait_recv()
                todo["cu"][p].wait_recv()
                total = kept(level, half, 3, p)
                total = total + land[level, half, 1, piece(p)].astype(F32)
                use(p, total + land[level, half, 2, piece(p)].astype(F32))

    def hold(p, total):
        held[piece(p)] = total

    parts = gather_start(0)
    table_copy = send(wanted, table_in, to_high)
    pool_load.wait()
    zbuf[pl.ds(z * SLOTS, SLOTS)] = pool_in[...].astype(BF)
    mine = zbuf.at[pl.ds(z * SLOTS, SLOTS)]
    state_copies = [send(mine, mine, device) for device in to_z]
    for level in range(L):
        small_weights(level)
    table_copy.wait_recv()
    table_load = load(table_in, table)
    table_load.wait()
    table_waits = [table_load]

    def states_across():
        for copy in state_copies:
            copy.wait_recv()
        crossing = []
        for entry in range(2 * L):
            asked = table[entry, 0]
            xsend[entry] = zbuf[(asked // (2 * SLOTS)) * SLOTS + asked % SLOTS]
            crossing.append(send(xsend.at[entry], xland.at[entry], to_high))
        return crossing

    for level in range(L):
        if level:
            parts = gather_start(level)
        parts["own"].wait_recv()
        for copy in weight_loads[level]:
            copy.wait()
        project_chunk(level, y)
        gather_near(level, parts)
        parts["down"].wait_recv()
        project_chunk(level, down)
        gather_far(level, parts)
        parts["up"].wait_recv()
        project_chunk(level, up)
        parts["far1"].wait_recv()
        parts["far2"].wait_recv()
        project_chunk(level, far)
        mix_blocks(level, x)
        if level == 0:
            crossing = states_across()
        gather_rest(level, parts)
        if level == 0:
            for copy in crossing:
                copy.wait_recv()
        mix_states(level, x)
        out_loads[level].wait()
        near = scatter_start(level, 0)
        parts["across"].wait_recv()
        for name in ("p3s", "m3s", "x2s"):
            parts[name].wait_recv()
        project_request(level, other)
        mix_blocks(level, other)
        scatter_middle(level, 0, near)
        mix_states(level, other)
        away = scatter_start(level, 1)
        scatter_end(level, 0, near, hold)
        scatter_middle(level, 1, away)
        last = [None] * PIECES

        def cross(p, total):
            sib[level, 1, 3, piece(p)] = total.astype(BF)
            last[p] = send(sib.at[level, 1, 3, piece(p)], last_land.at[level, piece(p)], to_x)

        scatter_end(level, 1, away, cross)
        for p in (0, 2, 1, 3):
            last[p].wait_recv()
            total = held[piece(p)] + last_land[level, piece(p)].astype(F32)
            current[piece(p)] = (current[piece(p)].astype(F32) + total).astype(BF)
    out_rows[...] = current[...]
    for copy in copies:
        copy.wait_send()


def run_layers(
    tokens, in_gain, w_query, w_key, w_value, w_gate, w_beta, w_decay,
    conv_query, conv_key, conv_value, a_log, dt_bias, out_gain, w_out,
    pool, owner, slot, lengths,
):
    wanted = (owner * SLOTS + slot).reshape(2 * L, 1)
    wanted = jnp.broadcast_to(jnp.pad(wanted, ((0, 8 - 2 * L), (0, 0))), (8, 128))
    vmem = pl.BlockSpec(memory_space=pltpu.VMEM)
    smem = pl.BlockSpec(memory_space=pltpu.SMEM)
    hbm = pl.BlockSpec(memory_space=pl.ANY)
    requests = lengths.shape[0]
    scratch = pltpu.VMEM
    return pl.pallas_call(
        layers_kernel,
        name="layers",
        in_specs=[
            vmem, vmem, hbm, hbm, hbm, hbm, vmem, vmem, vmem, vmem, vmem, smem, smem, vmem,
            hbm, hbm, smem, smem, smem, vmem,
        ],
        out_specs=[vmem, vmem],
        out_shape=[
            jax.ShapeDtypeStruct((ROWS, D), BF),
            jax.ShapeDtypeStruct((requests, L, HEADS, DK, DV), F32),
        ],
        scratch_shapes=[
            scratch((L, D, WIDE + 128), BF),
            scratch((L, HEADS * DV, D), BF),
            scratch((L, 16, ROWS, D), BF),
            scratch((2, PAD + SUF, DK), F32),
            scratch((2, PAD + SUF, DK), F32),
            scratch((2, PAD + SUF, HEADS * DV), F32),
            scratch((2, SUF, HEADS * DV), F32),
            scratch((2, SUF, 128), F32),
            scratch((BLOCKS, HEADS, 2 * CHUNK, DK), BF),
            scratch((BLOCKS, HEADS, 2 * CHUNK, DV), F32),
            scratch((BLOCKS, HEADS, 8, DV), F32),
            scratch((SUF, HEADS * DV), BF),
            scratch((L, 2, 4, 2 * ROWS, D), BF),
            scratch((L, 2, 4, ROWS, D), BF),
            scratch((L, 2, 3, ROWS, D), BF),
            scratch((L, ROWS, D), BF),
            scratch((ROWS, D), F32),
            scratch((ROWS, D), BF),
            scratch((SLOTS, HEADS, DK, DV), F32),
            scratch((4 * SLOTS, HEADS, DK, DV), BF),
            scratch((2 * L, HEADS, DK, DV), BF),
            scratch((2 * L, HEADS, DK, DV), BF),
            scratch((8, 128), jnp.int32),
            pltpu.SMEM((8, 128), jnp.int32),
            pltpu.SemaphoreType.DMA((SEMS,)),
            pltpu.SemaphoreType.DMA((SEMS,)),
            pltpu.SemaphoreType.DMA((16,)),
        ],
        compiler_params=pltpu.CompilerParams(
            collective_id=0, has_side_effects=True, vmem_limit_bytes=60 * 1024 * 1024
        ),
    )(
        tokens, in_gain, w_query, w_key, w_value, w_gate,
        w_beta.transpose(0, 2, 1), w_decay.transpose(0, 2, 1),
        conv_query, conv_key, conv_value, a_log, dt_bias, out_gain, w_out,
        pool, owner, slot, lengths, wanted,
    )


def solution(mesh):
    heads = P(None, None, "head")
    in_specs = (
        P(("req", "head"), None), P(), heads, heads, heads, heads, heads, heads,
        heads, heads, heads, P(None, "head"), P(None, "head"), P(),
        P(None, "head", None), P("req", "head", None, None),
        P("req", None), P("req", None), P("req"),
    )
    out_specs = (P(("req", "head"), None), P("req", None, "head", None, None))

    def on_device(*arrays):
        return tuple(run_layers(*arrays))

    return jax.shard_map(
        on_device, mesh=mesh, in_specs=in_specs, out_specs=out_specs, check_vma=False
    )
```

time: 367 us -> 125 us (0.34)
  waiting for transfers between devices: 253 us -> 0 us
  Pallas kernels: 55.1 us -> 119 us
  matrix products: 23.5 us -> 0 us
  between operations: 14 us -> 0.64 us
  other arithmetic: 10.2 us -> 0.7 us
  local copies, waits for them, and re-layouts: 9.25 us -> 4.3 us
    reduce_scatter x2 -> x0, waiting for transfers between devices: 132 us -> none  [branch(): lax.psum_scatter(dot(mixed, w_out[level]).astype(BF), 'head', scatter_dim...]
    all_gather x3 -> x0, waiting for transfers between devices: 121 us -> none  [the longest x2 72.1 us: branch(): everyone = lax.all_gather(normed, 'head', axis=0, tiled=True)]
    pallas_call x2 -> x1, Pallas kernels: 55.1 us -> 119 us  [run_layers(): pl.pallas_call(layers_kernel, name='layers', in_specs=[vmem, vmem, hbm, h...]
    dot_general x12 -> x0, matrix products: 23.5 us -> none  [the longest x10 21.2 us: dot(): return jnp.dot(a, b, preferred_element_type=F32)]
    convert_element_type x5 -> x0, other arithmetic: 7.22 us -> none  [the longest x2 3.56 us: branch(): normed = normalize(rows_in, in_gain[level]).astype(BF)]
  transfers between devices with their start and end apart: 5 -> 0, of which waited for: 5 -> 0; matrix products, arithmetic and copies ran while one was open for 3% -> 0% of each run, Pallas kernels for 0% -> 0%
where the time goes in v2:
time: 125 us
  Pallas kernels  119 us (95%)
  local copies, waits for them, and re-layouts  4.3 us (3%)
    pallas_call x1, Pallas kernels, run_layers(): pl.pallas_call(layers_kernel, name='layers', in_specs=[vmem, vmem, hbm, h...  119 us
    unnamed x2, local copies, waits for them, and re-layouts  3.54 us

profile of v2, /device:TPU:2, one launch (start us, length us, event | category | flops | bytes accessed | tf_op | source)
XLA Modules:
  0.0 124.5 jit_solution(3032420838506069820)
XLA Ops:
  0.6 0.7 multiply_add_fusion
  1.3 0.1 reshape.7
  1.4 0.7 broadcast_in_dim.8.wanted
  2.1 118.9 %layers.1 = (bf16[64,2048]{1,0:T(8,128)(2,1)}, f32[2,2,2,128,128]{4,3,2,1,0:T(8,128)}) custom-call(bf16[64,2048]{1,0:T(8,128)(2,1)} %tokens.1, f32[2,2048]{1,0:T(2,128)} %in_gain.1, bf16[2,2048,128]{2,1,0:T(8,128)(2,1)} %w_query.1, bf16[2,2048,128]{2,1,0:T(8,128)(2,1)} %w_key.1, bf16[2,2048,256]{2,1,0:T(8,128)(2,1)} %w_value.1, ...), custom_call_target="tpu_custom_call" | custom-call | tf_op jit(solution)/shard_map/layers/pallas_call | solution.py:509
  121.0 1.7 %copy.23 = bf16[64,2048]{1,0:T(8,128)(2,1)} copy(bf16[64,2048]{1,0:T(8,128)(2,1)} %get-tuple-element.4) | data formatting | bytes 524288
  122.6 1.9 %copy.24 = f32[2,2,2,128,128]{4,3,2,1,0:T(8,128)} copy(f32[2,2,2,128,128]{4,3,2,1,0:T(8,128)} %get-tuple-element.5) | data formatting | bytes 1048576
  (1 shorter events, 0.0 us)

commit v3 on v2

v3 whole, which is shorter than its diff:
```python
import jax
import jax.numpy as jnp
from jax import lax
from jax.experimental import pallas as pl
from jax.experimental.pallas import tpu as pltpu
from jax.sharding import PartitionSpec as P

DK = 128
DV = 128
L = 2
SLOTS = 4
SUF = 512
CONV = 4
HEADS = 2
CHUNK = 128
BLOCKS = SUF // CHUNK
PAD = 8
EPS = 1e-06
BF = jnp.bfloat16
F32 = jnp.float32
D = 2048
ROWS = 64
PIECE = 16
PIECES = ROWS // PIECE
ORDER = (0, 2, 1, 3)
WIDE = 2 * DK + 2 * HEADS * DV
SEMS = 176


def silu(v):
    return v / (1.0 + jnp.exp(-v))


def conv_block(ref, row, width, taps):
    window = ref[pl.ds(row, CHUNK + PAD), 0:width]
    total = None
    for tap in range(CONV):
        first = PAD - (CONV - 1) + tap
        term = window[first : first + CHUNK] * taps[tap : tap + 1]
        total = term if total is None else total + term
    return silu(total)


def unit_rows(vectors):
    return vectors * lax.rsqrt(jnp.sum(vectors * vectors, -1, keepdims=True) + EPS)


def mm(a, b):
    return jnp.dot(a.astype(BF), b.astype(BF), preferred_element_type=F32)


def nt(a, b):
    return lax.dot_general(
        a.astype(BF), b.astype(BF), (((1,), (1,)), ((), ())), preferred_element_type=F32
    )


def lower_inverses(stricts, rows, cols):
    size = 16
    near = rows // size == cols // size
    eye = jnp.where(rows == cols, 1.0, 0.0)
    diags = [jnp.where(near, -strict, 0.0) for strict in stricts]
    inverses = [eye + diag for diag in diags]
    powers = [mm(diag, diag) for diag in diags]
    for _ in range(2):
        both = [
            mm(jnp.concatenate([power, inverse], 0), power)
            for power, inverse in zip(powers, inverses)
        ]
        inverses = [inverse + pair[CHUNK:] for inverse, pair in zip(inverses, both)]
        powers = [pair[:CHUNK] for pair in both]
    inverses = [inverse + mm(inverse, power) for inverse, power in zip(inverses, powers)]
    while size < CHUNK:
        joined = (rows // (2 * size) == cols // (2 * size)) & (rows // size > cols // size)
        halves = [
            mm(jnp.where(joined, strict, 0.0), inverse)
            for strict, inverse in zip(stricts, inverses)
        ]
        inverses = [inverse - mm(inverse, half) for inverse, half in zip(inverses, halves)]
        size *= 2
    return inverses


def gate_rows(raw, a_log, dt_bias, valid):
    rows = []
    for head in range(HEADS):
        rows.append(jnp.where(valid, 1.0 / (1.0 + jnp.exp(-raw[head : head + 1])), 0.0))
    for head in range(HEADS):
        shifted = raw[HEADS + head : HEADS + head + 1] + dt_bias[head]
        soft = jnp.maximum(shifted, 0.0) + jnp.log1p(jnp.exp(-jnp.abs(shifted)))
        rate = jnp.exp(jnp.full((1, CHUNK), a_log[head], F32))
        rows.append(jnp.where(valid, -rate * soft, 0.0))
    rows.append(jnp.zeros((8 - 2 * HEADS, CHUNK), F32))
    return jnp.concatenate(rows, 0)


def block_terms(blocks, q_ref, k_ref, v_ref, raws, taps, a_log, dt_bias, length, move_ref, add_ref, tail_ref):
    rows = lax.broadcasted_iota(jnp.int32, (CHUNK, CHUNK), 0)
    cols = lax.broadcasted_iota(jnp.int32, (CHUNK, CHUNK), 1)
    lane = lax.broadcasted_iota(jnp.int32, (1, CHUNK), 1)
    upper = jnp.where(rows <= cols, 1.0, 0.0)
    gates = [
        gate_rows(raw, a_log, dt_bias, block * CHUNK + lane < length)
        for block, raw in zip(blocks, raws)
    ]
    sums = jnp.dot(
        jnp.concatenate(gates, 0), upper, precision=lax.Precision.HIGHEST, preferred_element_type=F32
    )
    sums = [sums[8 * index : 8 * index + 8] for index in range(len(blocks))]
    columns = [jnp.concatenate([gate, total], 0).T for gate, total in zip(gates, sums)]
    keys = [unit_rows(conv_block(k_ref, block * CHUNK, DK, taps[1])) for block in blocks]
    queries = [
        unit_rows(conv_block(q_ref, block * CHUNK, DK, taps[0])) * DK ** (-0.5) for block in blocks
    ]
    dots = [nt(jnp.concatenate([key, query], 0), key) for key, query in zip(keys, queries)]
    units = [(index, head) for index in range(len(blocks)) for head in range(HEADS)]
    stricts, decays = [], []
    for index, head in units:
        cumul = columns[index][:, 8 + HEADS + head : 9 + HEADS + head]
        cumul_row = sums[index][HEADS + head : HEADS + head + 1]
        decay = jnp.where(rows >= cols, jnp.exp(jnp.minimum(cumul - cumul_row, 0.0)), 0.0)
        beta = columns[index][:, head : head + 1]
        stricts.append(jnp.where(rows > cols, dots[index][:CHUNK] * decay * beta, 0.0))
        decays.append(decay)
    inverses = lower_inverses(stricts, rows, cols)
    values = [conv_block(v_ref, block * CHUNK, HEADS * DV, taps[2]) for block in blocks]
    solved = []
    for (index, head), inverse in zip(units, inverses):
        beta = columns[index][:, head : head + 1]
        grown = jnp.exp(columns[index][:, 8 + HEADS + head : 9 + HEADS + head])
        right = jnp.concatenate(
            [values[index][:, head * DV : (head + 1) * DV] * beta, keys[index] * (beta * grown)], 1
        )
        solved.append(mm(inverse, right))
    for (index, head), decay, solution_now in zip(units, decays, solved):
        cumul = columns[index][:, 8 + HEADS + head : 9 + HEADS + head]
        last = cumul[CHUNK - 1 :]
        key_tail = keys[index] * jnp.exp(last - cumul)
        mixing = dots[index][CHUNK:] * decay
        both = mm(jnp.concatenate([key_tail.T, mixing], 0), solution_now)
        move = jnp.concatenate(
            [-both[:DK, DV:], queries[index] * jnp.exp(cumul) - both[DK:, DV:]], 0
        )
        move_ref[blocks[index], head] = move.astype(BF)
        add_ref[blocks[index], head] = both[:, :DV]
        tail_ref[blocks[index], head] = jnp.broadcast_to(jnp.exp(last), (8, DV))


def run_states(start, move_ref, add_ref, tail_ref, z_ref, gain, length, store):
    states = [start[head] for head in range(HEADS)]
    for block in range(BLOCKS):
        place = block * CHUNK + lax.broadcasted_iota(jnp.int32, (CHUNK, 1), 0)
        valid = (place < length).astype(F32)
        results = [
            mm(move_ref[block, head], states[head]) + add_ref[block, head] for head in range(HEADS)
        ]
        for head in range(HEADS):
            states[head] = tail_ref[block, head][0:1] * states[head] + results[head][:DK]
            out = results[head][DK:]
            scale = lax.rsqrt(jnp.mean(out * out, -1, keepdims=True) + EPS)
            gate = z_ref[pl.ds(block * CHUNK, CHUNK), head * DV : (head + 1) * DV]
            store(block, head, (out * scale * gain * silu(gate) * valid).astype(BF))
    return states


def spot(x, y, core):
    return x * 8 + y * 2 + core


def piece(index):
    return pl.ds(index * PIECE, PIECE)


def layers_kernel(
    tokens, in_gain_hbm, w_query, w_key, w_value, w_gate, w_beta_hbm, w_decay_hbm,
    conv_query_hbm, conv_key_hbm, conv_value_hbm, a_log_hbm, dt_bias_hbm, out_gain_hbm, w_out,
    pool, owner_hbm, slot_hbm, lengths_hbm,
    out_rows, final_hbm,
    weights, outs, buf, q_ref, k_ref, v_ref, z_ref, raw_ref, move_ref, add_ref, tail_ref,
    mixed, stage, sib, land, current, pool_in, zbuf, xsend, xland,
    wanted, table_in, table, in_gain, w_beta, w_decay, conv_query, conv_key, conv_value, out_gain,
    a_log, dt_bias, owner, slot, lengths, final, send_sems, recv_sems, local_sems,
):
    me = lax.axis_index("head")
    group = lax.axis_index("req")
    x, y, core = me // 8, (me // 2) % 4, me % 2
    z, high = group // 2, group % 2
    other, up, down, far = 1 - x, (y + 1) % 4, (y + 3) % 4, (y + 2) % 4
    middle = PIECES // 2

    to_x = {"head": spot(other, y, core)}
    to_up, to_down = {"head": spot(x, up, core)}, {"head": spot(x, down, core)}
    sibling = {"head": spot(x, y, 1 - core)}
    to_high = {"req": z * 2 + 1 - high}
    to_z = [{"req": ((z + step) % 4) * 2 + high} for step in (1, 3, 2)]

    count = [0]

    def remote(source, target, device):
        index = count[0]
        count[0] += 1
        return pltpu.make_async_remote_copy(
            src_ref=source,
            dst_ref=target,
            send_sem=send_sems.at[index],
            recv_sem=recv_sems.at[index],
            device_id=device,
            device_id_type=pl.DeviceIdType.MESH,
        )

    def same(ref, device):
        return remote(ref, ref, device)

    class Moves:
        def __init__(self, level, request):
            def block(b):
                return buf.at[level, spot(request, b, core)]

            def part(b, p):
                return buf.at[level, spot(request, b, core), piece(p)]

            halves = [pl.ds(0, ROWS // 2), pl.ds(ROWS // 2, ROWS // 2)]
            self.across = []
            if level == 0:
                self.across = [same(current.at[request, piece(p)], to_x) for p in range(PIECES)]
            self.ups = [same(part(y, p), to_up) for p in range(PIECES)]
            self.downs = [same(part(y, p), to_down) for p in range(PIECES)]
            self.fars = [
                same(part(down, p), to_up) if p < middle else same(part(up, p), to_down)
                for p in range(PIECES)
            ]
            self.own_core = same(block(y), sibling)
            self.down_core = same(block(down), sibling)
            self.up_core = same(block(up), sibling)
            self.far_core = [
                same(buf.at[level, spot(request, far, core), rows], sibling) for rows in halves
            ]
            here = (level, request)
            theirs = pl.ds(pl.multiple_of((1 - core) * ROWS, ROWS), ROWS)
            self.pairs = [
                remote(stage.at[(*here, index, theirs)], sib.at[(*here, index)], sibling)
                for index in range(4)
            ]

            def part_sum(index, p, device):
                return remote(
                    sib.at[(*here, index, piece(p))], land.at[(*here, index, piece(p))], device
                )

            self.far_sums = [
                part_sum(0, p, to_down if p < middle else to_up) for p in range(PIECES)
            ]
            self.down_sums = [part_sum(1, p, to_down) for p in range(PIECES)]
            self.up_sums = [part_sum(2, p, to_up) for p in range(PIECES)]
            self.cross_sums = [part_sum(3, p, to_x) for p in range(PIECES)]

        def always(self):
            return (
                self.ups + self.downs + self.fars
                + [self.own_core, self.down_core, self.up_core] + self.far_core
                + self.pairs + self.far_sums + self.down_sums + self.up_sums
            )

    moves = [[Moves(level, request) for request in range(2)] for level in range(L)]

    loads, stores = [], []

    def load(source, target):
        copy = pltpu.make_async_copy(source, target, local_sems.at[len(loads)])
        copy.start()
        loads.append(copy)
        return copy

    open_loads = [load(tokens, current.at[x]), load(in_gain_hbm, in_gain)]
    pool_loads = [load(owner_hbm, owner), load(slot_hbm, slot), load(pool, pool_in)]
    small_loads = [load(w_beta_hbm, w_beta), load(w_decay_hbm, w_decay)]
    mix_loads = [
        load(source, target)
        for source, target in (
            (conv_query_hbm, conv_query), (conv_key_hbm, conv_key), (conv_value_hbm, conv_value),
            (a_log_hbm, a_log), (dt_bias_hbm, dt_bias), (out_gain_hbm, out_gain),
            (lengths_hbm, lengths),
        )
    ]
    weight_loads, out_loads = [], []
    for level in range(L):
        first = 0
        mine = []
        for source, width in (
            (w_query, DK), (w_key, DK), (w_value, HEADS * DV), (w_gate, HEADS * DV),
        ):
            mine.append(load(source.at[level], weights.at[level, :, pl.ds(first, width)]))
            first += width
        weight_loads.append(mine)
        out_loads.append(load(w_out.at[level], outs.at[level]))

    barrier = pltpu.get_barrier_semaphore()
    partners = [to_x, to_up, to_down, sibling, to_high] + to_z
    for partner in partners:
        pl.semaphore_signal(
            barrier, inc=1, device_id=partner, device_id_type=pl.DeviceIdType.MESH
        )
    pl.semaphore_wait(barrier, len(partners))
    for copy in open_loads:
        copy.wait()

    def spread_piece(level, request, p):
        floats = current[request, piece(p)].astype(F32)
        scale = lax.rsqrt(jnp.mean(floats * floats, -1, keepdims=True) + EPS)
        normed = (floats * scale * in_gain[level : level + 1]).astype(BF)
        buf[level, spot(request, y, core), piece(p)] = normed
        moves[level][request].ups[p].start()
        moves[level][request].downs[p].start()

    def open_request(request):
        move = moves[0][request]
        for p in ORDER:

            @pl.when(x != request)
            def _():
                move.across[p].wait_recv()

            spread_piece(0, request, p)
        move.own_core.start()

    def gather_near(level, request):
        move = moves[level][request]
        for p in ORDER:
            move.ups[p].wait_recv()
            if p < middle:
                move.fars[p].start()
            move.downs[p].wait_recv()
            if p >= middle:
                move.fars[p].start()
        move.down_core.start()
        move.up_core.start()

    def gather_far(level, request):
        move = moves[level][request]
        for first in (0, middle):
            for p in range(first, first + middle):
                move.fars[p].wait_recv()
            move.far_core[first // middle].start()

    def small_weights(level):
        rows = jnp.concatenate(
            [
                w_beta[level].astype(F32),
                w_decay[level].astype(F32),
                jnp.zeros((128 - 2 * HEADS, D), F32),
            ],
            0,
        )
        weights[level, :, WIDE:] = rows.T.astype(BF)

    def keep(request, result, row, rows):
        place = pl.ds(row + PAD, rows)
        q_ref[request, place] = result[:, 0:DK]
        k_ref[request, place] = result[:, DK : 2 * DK]
        v_ref[request, place] = result[:, 2 * DK : 2 * DK + HEADS * DV]
        z_ref[request, pl.ds(row, rows)] = result[:, 2 * DK + HEADS * DV : WIDE]
        raw_ref[request, pl.ds(row, rows)] = result[:, WIDE:]

    def project_chunk(level, request, b):
        rows = buf[level, pl.ds(spot(request, b, 0), 2)].reshape(CHUNK, D)
        result = jnp.dot(rows, weights[level], preferred_element_type=F32)
        keep(request, result, pl.multiple_of(b * CHUNK, CHUNK), CHUNK)

    def project_request(level, request):
        rows = buf[level, pl.ds(request * 8, 8)].reshape(SUF, D)
        result = jnp.dot(rows, weights[level], preferred_element_type=F32)
        keep(request, result, 0, SUF)

    def mix_blocks(level, request):
        blocks = list(range(BLOCKS))
        raws = [
            raw_ref[request, pl.ds(block * CHUNK, CHUNK)].T[0 : 2 * HEADS] for block in blocks
        ]
        block_terms(
            blocks, q_ref.at[request], k_ref.at[request], v_ref.at[request], raws,
            (conv_query[level], conv_key[level], conv_value[level]),
            [a_log[level, head] for head in range(HEADS)],
            [dt_bias[level, head] for head in range(HEADS)],
            lengths[request], move_ref, add_ref, tail_ref,
        )

    def mix_states(level, request):
        holder = owner[request, level]
        near = zbuf[(holder // 2) * SLOTS + slot[request, level]]
        start = jnp.where(holder % 2 == high, near, xland[request * L + level]).astype(F32)

        def store(block, head, rows):
            mixed[pl.ds(block * CHUNK, CHUNK), head * DV : (head + 1) * DV] = rows

        states = run_states(
            start, move_ref, add_ref, tail_ref, z_ref.at[request], out_gain[level : level + 1],
            lengths[request], store,
        )
        for head in range(HEADS):
            final[request, level, head] = states[head]
        stores.append(load(final.at[request, level], final_hbm.at[request, level]))

    def kept(level, request, index, p):
        row = pl.multiple_of(core * ROWS + p * PIECE, PIECE)
        mine = stage[level, request, index, pl.ds(row, PIECE)].astype(F32)
        return mine + sib[level, request, index, piece(p)].astype(F32)

    def scatter_start(level, request):
        move = moves[level][request]

        def term(index, b):
            rows = mixed[pl.ds(pl.multiple_of(b * CHUNK, CHUNK), CHUNK)]
            stage[level, request, index] = jnp.dot(
                rows, outs[level], preferred_element_type=F32
            ).astype(BF)
            move.pairs[index].start()

        def pass_on(index, p, copy):
            sib[level, request, index, piece(p)] = kept(level, request, index, p).astype(BF)
            copy.start()

        term(0, far)
        term(1, down)
        term(2, up)
        move.pairs[0].wait_recv()
        for p in range(middle):
            pass_on(0, p, move.far_sums[p])
            pass_on(0, p + middle, move.far_sums[p + middle])
        term(3, y)
        move.pairs[1].wait_recv()
        move.pairs[2].wait_recv()
        for p in range(middle):
            pass_on(1, p + middle, move.down_sums[p + middle])
            pass_on(2, p, move.up_sums[p])
        move.pairs[3].wait_recv()

    def scatter_middle(level, request):
        move = moves[level][request]
        for step in range(middle):
            for p, index, sums in (
                (step, 1, move.down_sums), (step + middle, 2, move.up_sums),
            ):
                move.far_sums[p].wait_recv()
                total = kept(level, request, index, p)
                total = total + land[level, request, 0, piece(p)].astype(F32)
                sib[level, request, index, piece(p)] = total.astype(BF)
                sums[p].start()

    def scatter_end(level, request):
        move = moves[level][request]
        for p in ORDER:
            move.down_sums[p].wait_recv()
            move.up_sums[p].wait_recv()
            total = kept(level, request, 3, p)
            total = total + land[level, request, 1, piece(p)].astype(F32)
            total = total + land[level, request, 2, piece(p)].astype(F32)
            sib[level, request, 3, piece(p)] = total.astype(BF)
            if level + 1 < L:
                move.cross_sums[p].start()
            else:

                @pl.when(x != request)
                def _():
                    move.cross_sums[p].start()

    def add_piece(level, request, p):
        moves[level][request].cross_sums[p].wait_recv()
        total = sib[level, request, 3, piece(p)].astype(F32)
        total = total + land[level, request, 3, piece(p)].astype(F32)
        old = current[request, piece(p)].astype(F32)
        current[request, piece(p)] = (old + total).astype(BF)

    def next_rows(level, request):
        if level + 1 < L:

            @pl.when(x == request)
            def _():
                for copy in moves[level][request].across:
                    copy.wait_send()

            for p in ORDER:
                add_piece(level, request, p)
                spread_piece(level + 1, request, p)
            moves[level + 1][request].own_core.start()
        else:

            @pl.when(x == request)
            def _():
                for p in ORDER:
                    add_piece(level, request, p)

    for request in range(2):

        @pl.when(x == request)
        def _():
            for p in ORDER:
                moves[0][request].across[p].start()

    open_request(0)

    for copy in pool_loads:
        copy.wait()
    entry_rows = lax.broadcasted_iota(jnp.int32, (8, 128), 0)
    asks = jnp.zeros((8, 128), jnp.int32)
    for entry in range(2 * L):
        row = owner[entry // L, entry % L] * SLOTS + slot[entry // L, entry % L]
        asks = jnp.where(entry_rows == entry, row, asks)
    wanted[...] = asks
    table_copy = remote(wanted, table_in, to_high)
    table_copy.start()
    zbuf[pl.ds(z * SLOTS, SLOTS)] = pool_in[...].astype(BF)
    state_copies = [same(zbuf.at[pl.ds(z * SLOTS, SLOTS)], device) for device in to_z]
    for copy in state_copies[:2]:
        copy.start()
    for ref in (q_ref, k_ref, v_ref):
        ref[:, 0:PAD] = jnp.zeros((2, PAD, ref.shape[2]), F32)
    for copy in small_loads:
        copy.wait()
    small_weights(0)
    for copy in mix_loads:
        copy.wait()
    crossing = [remote(xsend.at[entry], xland.at[entry], to_high) for entry in range(2 * L)]

    def states_across():
        table_copy.wait_recv()
        table_load = load(table_in, table)
        for copy in state_copies:
            copy.wait_recv()
        table_load.wait()
        for entry in range(2 * L):
            asked = table[entry, 0]
            xsend[entry] = zbuf[(asked // (2 * SLOTS)) * SLOTS + asked % SLOTS]
            crossing[entry].start()

    for level in range(L):
        if level:
            scatter_end(0, 0)
            scatter_middle(0, 1)
            next_rows(0, 0)
            scatter_end(0, 1)
        for copy in weight_loads[level]:
            copy.wait()
        move = moves[level][0]
        move.own_core.wait_recv()
        project_chunk(level, 0, y)
        gather_near(level, 0)
        if level:
            next_rows(0, 1)
        else:
            state_copies[2].start()
            open_request(1)
        move.down_core.wait_recv()
        project_chunk(level, 0, down)
        gather_far(level, 0)
        move.up_core.wait_recv()
        project_chunk(level, 0, up)
        for copy in move.far_core:
            copy.wait_recv()
        project_chunk(level, 0, far)
        gather_near(level, 1)
        if level == 0:
            states_across()
        mix_blocks(level, 0)
        gather_far(level, 1)
        if level == 0:
            for copy in crossing:
                copy.wait_recv()
            small_weights(1)
        mix_states(level, 0)
        out_loads[level].wait()
        scatter_start(level, 0)
        move = moves[level][1]
        for copy in [move.own_core, move.down_core, move.up_core] + move.far_core:
            copy.wait_recv()
        project_request(level, 1)
        mix_blocks(level, 1)
        scatter_middle(level, 0)
        mix_states(level, 1)
        scatter_start(level, 1)
    scatter_end(1, 0)
    scatter_middle(1, 1)
    next_rows(1, 0)
    scatter_end(1, 1)
    next_rows(1, 1)
    stores.append(load(current.at[x], out_rows))
    for copy in stores:
        copy.wait()
    for copy in [table_copy] + state_copies + crossing:
        copy.wait_send()
    for level in range(L):
        for request in range(2):
            move = moves[level][request]
            for copy in move.always():
                copy.wait_send()

            if level == 0:
                for copy in move.cross_sums:
                    copy.wait_send()
            else:

                @pl.when(x != request)
                def _():
                    for copy in move.cross_sums:
                        copy.wait_send()


def run_layers(
    tokens, in_gain, w_query, w_key, w_value, w_gate, w_beta, w_decay,
    conv_query, conv_key, conv_value, a_log, dt_bias, out_gain, w_out,
    pool, owner, slot, lengths,
):
    requests = lengths.shape[0]
    scratch = pltpu.VMEM
    return pl.pallas_call(
        layers_kernel,
        name="layers",
        in_specs=[pl.BlockSpec(memory_space=pl.ANY)] * 19,
        out_specs=[pl.BlockSpec(memory_space=pl.ANY)] * 2,
        out_shape=[
            jax.ShapeDtypeStruct((ROWS, D), BF),
            jax.ShapeDtypeStruct((requests, L, HEADS, DK, DV), F32),
        ],
        scratch_shapes=[
            scratch((L, D, WIDE + 128), BF),
            scratch((L, HEADS * DV, D), BF),
            scratch((L, 16, ROWS, D), BF),
            scratch((2, PAD + SUF, DK), F32),
            scratch((2, PAD + SUF, DK), F32),
            scratch((2, PAD + SUF, HEADS * DV), F32),
            scratch((2, SUF, HEADS * DV), F32),
            scratch((2, SUF, 128), F32),
            scratch((BLOCKS, HEADS, 2 * CHUNK, DK), BF),
            scratch((BLOCKS, HEADS, 2 * CHUNK, DV), F32),
            scratch((BLOCKS, HEADS, 8, DV), F32),
            scratch((SUF, HEADS * DV), BF),
            scratch((L, 2, 4, 2 * ROWS, D), BF),
            scratch((L, 2, 4, ROWS, D), BF),
            scratch((L, 2, 4, ROWS, D), BF),
            scratch((2, ROWS, D), BF),
            scratch((SLOTS, HEADS, DK, DV), F32),
            scratch((4 * SLOTS, HEADS, DK, DV), BF),
            scratch((2 * L, HEADS, DK, DV), BF),
            scratch((2 * L, HEADS, DK, DV), BF),
            scratch((8, 128), jnp.int32),
            scratch((8, 128), jnp.int32),
            pltpu.SMEM((8, 128), jnp.int32),
            scratch((L, D), F32),
            scratch((L, HEADS, D), BF),
            scratch((L, HEADS, D), BF),
            scratch((L, CONV, DK), F32),
            scratch((L, CONV, DK), F32),
            scratch((L, CONV, HEADS * DV), F32),
            scratch((L, DV), F32),
            pltpu.SMEM((L, HEADS), F32),
            pltpu.SMEM((L, HEADS), F32),
            pltpu.SMEM((requests, L), jnp.int32),
            pltpu.SMEM((requests, L), jnp.int32),
            pltpu.SMEM((requests,), jnp.int32),
            scratch((requests, L, HEADS, DK, DV), F32),
            pltpu.SemaphoreType.DMA((SEMS,)),
            pltpu.SemaphoreType.DMA((SEMS,)),
            pltpu.SemaphoreType.DMA((40,)),
        ],
        compiler_params=pltpu.CompilerParams(
            collective_id=0, has_side_effects=True, vmem_limit_bytes=60 * 1024 * 1024
        ),
    )(
        tokens, in_gain, w_query, w_key, w_value, w_gate,
        w_beta.transpose(0, 2, 1), w_decay.transpose(0, 2, 1),
        conv_query, conv_key, conv_value, a_log, dt_bias, out_gain, w_out,
        pool, owner, slot, lengths,
    )


def solution(mesh):
    heads = P(None, None, "head")
    in_specs = (
        P(("req", "head"), None), P(), heads, heads, heads, heads, heads, heads,
        heads, heads, heads, P(None, "head"), P(None, "head"), P(),
        P(None, "head", None), P("req", "head", None, None),
        P("req", None), P("req", None), P("req"),
    )
    out_specs = (P(("req", "head"), None), P("req", None, "head", None, None))

    def on_device(*arrays):
        return tuple(run_layers(*arrays))

    return jax.shard_map(
        on_device, mesh=mesh, in_specs=in_specs, out_specs=out_specs, check_vma=False
    )
```

time: 125 us -> 112 us (0.90)
  Pallas kernels: 119 us -> 108 us
    pallas_call x1, Pallas kernels: 119 us -> 108 us  [run_layers(): pl.pallas_call(layers_kernel, name='layers', in_specs=[pl.BlockSpec(memor...]
where the time goes in v3:
time: 112 us
  Pallas kernels  108 us (96%)
  local copies, waits for them, and re-layouts  3.54 us (3%)
    pallas_call x1, Pallas kernels, run_layers(): pl.pallas_call(layers_kernel, name='layers', in_specs=[pl.BlockSpec(memor...  108 us
    unnamed x2, local copies, waits for them, and re-layouts  3.54 us

profile of v3, /device:TPU:2, one launch (start us, length us, event | category | flops | bytes accessed | tf_op | source)
XLA Modules:
  0.0 112.3 jit_solution(10580661068351487963)
XLA Ops:
  0.6 108.1 %layers.1 = (bf16[64,2048]{1,0:T(8,128)(2,1)}, f32[2,2,2,128,128]{4,3,2,1,0:T(8,128)}) custom-call(bf16[64,2048]{1,0:T(8,128)(2,1)} %tokens.1, f32[2,2048]{1,0:T(2,128)} %in_gain_hbm.1, bf16[2,2048,128]{2,1,0:T(8,128)(2,1)} %w_query.1, bf16[2,2048,128]{2,1,0:T(8,128)(2,1)} %w_key.1, bf16[2,2048,256]{2,1,0:T(8,128)(2,1)} %w_value.1, ...), custom_call_target="tpu_custom_call" | custom-call | tf_op jit(solution)/shard_map/layers/pallas_call | solution.py:614
  108.7 1.7 %copy.23 = bf16[64,2048]{1,0:T(8,128)(2,1)} copy(bf16[64,2048]{1,0:T(8,128)(2,1)} %get-tuple-element.4) | data formatting | bytes 524288
  110.4 1.9 %copy.24 = f32[2,2,2,128,128]{4,3,2,1,0:T(8,128)} copy(f32[2,2,2,128,128]{4,3,2,1,0:T(8,128)} %get-tuple-element.5) | data formatting | bytes 1048576

commit v4 on v3

--- a/solution.py
+++ b/solution.py
@@ -534,6 +534,7 @@
 
     for level in range(L):
         if level:
+            small_weights(1)
             scatter_end(0, 0)
             scatter_middle(0, 1)
             next_rows(0, 0)
@@ -565,7 +566,6 @@
         if level == 0:
             for copy in crossing:
                 copy.wait_recv()
-            small_weights(1)
         mix_states(level, 0)
         out_loads[level].wait()
         scatter_start(level, 0)
@@ -602,6 +602,25 @@
                 def _():
                     for copy in move.cross_sums:
                         copy.wait_send()
+
+
+def hand_on_kernel(rows_in, states_in, rows_out, states_out):
+    rows_out[...] = rows_in[...]
+    states_out[...] = states_in[...]
+
+
+def hand_on(rows, states):
+    vmem = pl.BlockSpec(memory_space=pltpu.VMEM)
+    return pl.pallas_call(
+        hand_on_kernel,
+        name="hand_on",
+        in_specs=[vmem, vmem],
+        out_specs=[vmem, vmem],
+        out_shape=[
+            jax.ShapeDtypeStruct(rows.shape, rows.dtype),
+            jax.ShapeDtypeStruct(states.shape, states.dtype),
+        ],
+    )(rows, states)
 
 
 def run_layers(
@@ -683,7 +702,7 @@
     out_specs = (P(("req", "head"), None), P("req", None, "head", None, None))
 
     def on_device(*arrays):
-        return tuple(run_layers(*arrays))
+        return tuple(hand_on(*run_layers(*arrays)))
 
     return jax.shard_map(
         on_device, mesh=mesh, in_specs=in_specs, out_specs=out_specs, check_vma=False

time: 112 us -> 111 us (level)
  local copies, waits for them, and re-layouts: 3.54 us -> 0 us
  Pallas kernels: 108 us -> 110 us
    unnamed x2 -> x0, local copies, waits for them, and re-layouts: 3.54 us -> none
    pallas_call x0 -> x1, Pallas kernels: none -> 2.02 us  [hand_on(): pl.pallas_call(hand_on_kernel, name='hand_on', in_specs=[vmem, vmem], out...]
where the time goes in v4:
time: 111 us
  Pallas kernels  110 us (99%)
    pallas_call x1, Pallas kernels, run_layers(): pl.pallas_call(layers_kernel, name='layers', in_specs=[pl.BlockSpec(memor...  108 us

profile of v4, /device:TPU:2, one launch (start us, length us, event | category | flops | bytes accessed | tf_op | source)
XLA Modules:
  0.0 110.7 jit_solution(14111536329630481040)
XLA Ops:
  0.6 108.1 %layers.1 = (bf16[64,2048]{1,0:T(8,128)(2,1)}, f32[2,2,2,128,128]{4,3,2,1,0:T(8,128)}) custom-call(bf16[64,2048]{1,0:T(8,128)(2,1)} %tokens.1, f32[2,2048]{1,0:T(2,128)} %in_gain_hbm.1, bf16[2,2048,128]{2,1,0:T(8,128)(2,1)} %w_query.1, bf16[2,2048,128]{2,1,0:T(8,128)(2,1)} %w_key.1, bf16[2,2048,256]{2,1,0:T(8,128)(2,1)} %w_value.1, ...), custom_call_target="tpu_custom_call" | custom-call | tf_op jit(solution)/shard_map/layers/pallas_call | solution.py:633
  108.7 2.0 %hand_on.1 = (bf16[64,2048]{1,0:T(8,128)(2,1)}, f32[2,2,2,128,128]{4,3,2,1,0:T(8,128)}) custom-call(bf16[64,2048]{1,0:T(8,128)(2,1)} %get-tuple-element.4.rows_in, f32[2,2,2,128,128]{4,3,2,1,0:T(8,128)} %get-tuple-element.5.states_in), custom_call_target="tpu_custom_call" | custom-call | tf_op jit(solution)/shard_map/hand_on/pallas_call | solution.py:614

commit v5 on v4

--- a/solution.py
+++ b/solution.py
@@ -432,8 +432,6 @@
         for p in range(middle):
             pass_on(1, p + middle, move.down_sums[p + middle])
             pass_on(2, p, move.up_sums[p])
-        move.pairs[3].wait_recv()
-
     def scatter_middle(level, request):
         move = moves[level][request]
         for step in range(middle):
@@ -448,6 +446,7 @@
 
     def scatter_end(level, request):
         move = moves[level][request]
+        move.pairs[3].wait_recv()
         for p in ORDER:
             move.down_sums[p].wait_recv()
             move.up_sums[p].wait_recv()
@@ -579,8 +578,8 @@
         scatter_start(level, 1)
     scatter_end(1, 0)
     scatter_middle(1, 1)
+    scatter_end(1, 1)
     next_rows(1, 0)
-    scatter_end(1, 1)
     next_rows(1, 1)
     stores.append(load(current.at[x], out_rows))
     for copy in stores:

time: 111 us -> 107 us (0.964)
  Pallas kernels: 110 us -> 107 us
    pallas_call x1, Pallas kernels: 108 us -> 105 us  [run_layers(): pl.pallas_call(layers_kernel, name='layers', in_specs=[pl.BlockSpec(memor...]
where the time goes in v5:
time: 107 us
  Pallas kernels  107 us (100%)
    pallas_call x1, Pallas kernels, run_layers(): pl.pallas_call(layers_kernel, name='layers', in_specs=[pl.BlockSpec(memor...  105 us

profile of v5, /device:TPU:2, one launch (start us, length us, event | category | flops | bytes accessed | tf_op | source)
XLA Modules:
  0.0 107.2 jit_solution(8195657675412054747)
XLA Ops:
  0.6 104.5 %layers.1 = (bf16[64,2048]{1,0:T(8,128)(2,1)}, f32[2,2,2,128,128]{4,3,2,1,0:T(8,128)}) custom-call(bf16[64,2048]{1,0:T(8,128)(2,1)} %tokens.1, f32[2,2048]{1,0:T(2,128)} %in_gain_hbm.1, bf16[2,2048,128]{2,1,0:T(8,128)(2,1)} %w_query.1, bf16[2,2048,128]{2,1,0:T(8,128)(2,1)} %w_key.1, bf16[2,2048,256]{2,1,0:T(8,128)(2,1)} %w_value.1, ...), custom_call_target="tpu_custom_call" | custom-call | tf_op jit(solution)/shard_map/layers/pallas_call | solution.py:632
  105.2 2.0 %hand_on.1 = (bf16[64,2048]{1,0:T(8,128)(2,1)}, f32[2,2,2,128,128]{4,3,2,1,0:T(8,128)}) custom-call(bf16[64,2048]{1,0:T(8,128)(2,1)} %get-tuple-element.4.rows_in, f32[2,2,2,128,128]{4,3,2,1,0:T(8,128)} %get-tuple-element.5.states_in), custom_call_target="tpu_custom_call" | custom-call | tf_op jit(solution)/shard_map/hand_on/pallas_call | solution.py:613
